TPU v7x, 32 devices: a whole 2x2x4 slice. The times are simulated.
32 devices in a mesh: narrow: 2 (over core), wide: 16 (over z, y, x).
Axes of the slice: x: 2, y: 2, z: 4, core: 2. Of those that a mesh axis runs over, the one named last changes fastest.
Arguments:
- inputs: bfloat16 [64, 512, 768], P(('narrow', 'wide')), may hold values from -6 to 6
- documents: int32 [64, 512], P(('narrow', 'wide')), may hold values from 0 to 5, never falling along the last dimension, each value on 1 to 256 neighbouring positions
- mixing: bfloat16 [12, 512, 512], P(None, 'narrow'), may hold values from -9 to 9
- value_weight: bfloat16 [768, 768], P(None, 'narrow'), may hold values from -0.21875 to 0.21875
- output_weight: bfloat16 [768, 768], P('narrow'), may hold values from -0.875 to 0.875
- mixer_gain: bfloat16 [768], P('narrow'), may hold values from 0.099609375 to 1.8984375
- mixer_shift: bfloat16 [768], P('narrow'), may hold values from -3 to 3
- dense_gain: bfloat16 [768], P('narrow'), may hold values from 0.099609375 to 1.8984375
- dense_shift: bfloat16 [768], P('narrow'), may hold values from -3 to 3
- hidden_weight: bfloat16 [768, 3072], P('narrow', 'wide'), may hold values from -0.21875 to 0.21875
- hidden_bias: bfloat16 [3072], P('narrow'), may hold values from -3 to 3
- down_weight: bfloat16 [3072, 768], P('wide', 'narrow'), may hold values from -0.21875 to 0.21875
- down_bias: bfloat16 [768], P('narrow'), may hold values from -3 to 3
- cotangent: bfloat16 [64, 512, 768], P(('narrow', 'wide')), may hold values from -6 to 6
Outputs:
- result: bfloat16 [64, 512, 768], P(('narrow', 'wide'))
- inputs_gradient: bfloat16 [64, 512, 768], P(('narrow', 'wide'))
- mixing_gradient: float32 [12, 512, 512], P(None, 'narrow')
- value_gradient: float32 [768, 768], P(None, 'narrow')
- output_gradient: float32 [768, 768], P('narrow')
- mixer_gain_gradient: float32 [768], P('narrow')
- mixer_shift_gradient: float32 [768], P('narrow')
- dense_gain_gradient: float32 [768], P('narrow')
- dense_shift_gradient: float32 [768], P('narrow')
- hidden_gradient: float32 [768, 3072], P('narrow', 'wide')
- hidden_bias_gradient: float32 [3072], P('narrow')
- down_gradient: float32 [3072, 768], P('wide', 'narrow')
- down_bias_gradient: float32 [768], P('narrow')
Inputs may be any that keep to these rules, and one draw needn't show every extreme that they name: `documents`: document numbers never fall along a row; each document holds 1 to 256 tokens and one holds exactly 256.
All inputs are finite; a program needn't handle non-finite values.
Results may differ from a plain program's by a relative error of at most 0.02.
Values may be sent and summed in bfloat16 or wider, within the bound.
A program may use at most 256 MiB of HBM per device.

v0:
```python
import jax
import jax.numpy as jnp
from jax import lax
from jax.sharding import PartitionSpec as P

D = 768
HEADS = 12
HEAD = 64
SEQ = 512


epsilon = 1e-05


def normalize(matrix, norm_gain, norm_shift):
    average = jnp.mean(matrix, axis=-1, keepdims=True)
    center = matrix - average
    reciprocal = lax.rsqrt(jnp.mean(center * center, axis=-1, keepdims=True) + epsilon)
    unit_rows = center * reciprocal
    return (unit_rows * norm_gain + norm_shift, unit_rows, reciprocal)


def norm_back(slope_rows, unit_rows, reciprocal, norm_gain):
    tilted = slope_rows * norm_gain
    centered_slope = tilted - jnp.mean(tilted, axis=-1, keepdims=True)
    centered_slope = centered_slope - unit_rows * jnp.mean(
        tilted * unit_rows, axis=-1, keepdims=True
    )
    return (
        centered_slope * reciprocal,
        jnp.sum(slope_rows * unit_rows, axis=0),
        jnp.sum(slope_rows, axis=0),
    )


def contract_rows(left_side, right_side):
    return lax.dot_general(
        left_side, right_side, (((0,), (0,)), ((), ())), preferred_element_type=jnp.float32
    )


def times_transpose(left_side, right_side):
    return lax.dot_general(
        left_side, right_side, (((1,), (1,)), ((), ())), preferred_element_type=jnp.float32
    )


def row_chances(mixing_full, row_docs):
    same_doc = row_docs[:, None] == row_docs[None, :]
    scores = jnp.where(same_doc[None, :, :], mixing_full.astype(jnp.float32), -1e30)
    row_top = jnp.max(scores, axis=-1, keepdims=True)
    raised = jnp.exp(scores - row_top)
    return raised / jnp.sum(raised, axis=-1, keepdims=True)


def local(
    inputs,
    documents,
    mixing,
    value_weight,
    output_weight,
    mixer_gain,
    mixer_shift,
    dense_gain,
    dense_shift,
    hidden_weight,
    hidden_bias,
    down_weight,
    down_bias,
    cotangent,
):
    gathered = (
        lax.all_gather(mixing, "narrow", axis=1, tiled=True),
        lax.all_gather(value_weight, "narrow", axis=1, tiled=True),
        lax.all_gather(output_weight, "narrow", axis=0, tiled=True),
        lax.all_gather(mixer_gain, "narrow", axis=0, tiled=True),
        lax.all_gather(mixer_shift, "narrow", axis=0, tiled=True),
        lax.all_gather(dense_gain, "narrow", axis=0, tiled=True),
        lax.all_gather(dense_shift, "narrow", axis=0, tiled=True),
        lax.all_gather(hidden_bias, "narrow", axis=0, tiled=True),
        lax.all_gather(down_bias, "narrow", axis=0, tiled=True),
    )
    mixing_full, value_full, output_full = (gathered[0], gathered[1], gathered[2])
    gain_first = gathered[3].astype(jnp.float32)
    shift_first = gathered[4].astype(jnp.float32)
    gain_second = gathered[5].astype(jnp.float32)
    shift_second = gathered[6].astype(jnp.float32)
    bias_hidden = gathered[7].astype(jnp.float32)
    bias_down = gathered[8].astype(jnp.float32)
    halfway = (
        lax.all_gather(hidden_weight, "narrow", axis=0, tiled=True),
        lax.all_gather(down_weight, "narrow", axis=1, tiled=True),
    )
    hidden_full, down_full = (
        lax.all_gather(halfway[0], "wide", axis=1, tiled=True),
        lax.all_gather(halfway[1], "wide", axis=0, tiled=True),
    )
    row_count = inputs.shape[0]
    stream = inputs.reshape(row_count * SEQ, D).astype(jnp.float32)
    normed, unit_first, recip_first = normalize(stream, gain_first, shift_first)
    normed_low = normed.astype(jnp.bfloat16)
    values = jnp.dot(normed_low, value_full, preferred_element_type=jnp.float32).astype(
        jnp.bfloat16
    )
    value_rows = values.reshape(row_count, SEQ, D)

    def mix_one(bundle):
        row_values, row_docs = bundle
        chances_low = row_chances(mixing_full, row_docs).astype(jnp.bfloat16)
        per_head = row_values.reshape(SEQ, HEADS, HEAD)
        blended_row = jnp.einsum(
            "hij,jhd->ihd", chances_low, per_head, preferred_element_type=jnp.float32
        )
        return blended_row.reshape(SEQ, D).astype(jnp.bfloat16)

    blended = lax.map(mix_one, (value_rows, documents)).reshape(row_count * SEQ, D)
    middle = stream + jnp.dot(blended, output_full, preferred_element_type=jnp.float32)
    normed_two, unit_second, recip_second = normalize(middle, gain_second, shift_second)
    normed_two_low = normed_two.astype(jnp.bfloat16)
    hidden = jnp.dot(normed_two_low, hidden_full, preferred_element_type=jnp.float32) + bias_hidden
    activated, gelu_pull = jax.vjp(jax.nn.gelu, hidden)
    active = activated.astype(jnp.bfloat16)
    result = middle + jnp.dot(active, down_full, preferred_element_type=jnp.float32) + bias_down
    slope_low = cotangent.reshape(row_count * SEQ, D)
    slope_wide = slope_low.astype(jnp.float32)
    down_bias_sum = jnp.sum(slope_wide, axis=0)
    down_grad = contract_rows(active, slope_low)
    active_slope = times_transpose(slope_low, down_full)
    hidden_slope_wide = gelu_pull(active_slope)[0]
    hidden_slope = hidden_slope_wide.astype(jnp.bfloat16)
    hidden_bias_sum = jnp.sum(hidden_slope.astype(jnp.float32), axis=0)
    hidden_grad = contract_rows(normed_two_low, hidden_slope)
    normed_two_slope = times_transpose(hidden_slope, hidden_full)
    back_second, gain_second_sum, shift_second_sum = norm_back(
        normed_two_slope, unit_second, recip_second, gain_second
    )
    middle_slope = slope_wide + back_second
    attended_slope = middle_slope.astype(jnp.bfloat16)
    output_grad = contract_rows(blended, attended_slope)
    blended_slope = times_transpose(attended_slope, output_full).astype(jnp.bfloat16)

    def mix_back(running, bundle):
        row_values, row_docs, row_slope = bundle
        chances = row_chances(mixing_full, row_docs)
        per_head = row_values.reshape(SEQ, HEADS, HEAD)
        head_slope = row_slope.reshape(SEQ, HEADS, HEAD)
        chance_slope = jnp.einsum(
            "ihd,jhd->hij", head_slope, per_head, preferred_element_type=jnp.float32
        )
        score_slope = chances * (
            chance_slope - jnp.sum(chances * chance_slope, axis=-1, keepdims=True)
        )
        value_part = jnp.einsum(
            "hij,ihd->jhd",
            chances.astype(jnp.bfloat16),
            head_slope,
            preferred_element_type=jnp.float32,
        )
        return (running + score_slope, value_part.reshape(SEQ, D).astype(jnp.bfloat16))

    mixing_start = jnp.zeros((HEADS, SEQ, SEQ), jnp.float32)
    mixing_grad, value_slopes = lax.scan(
        mix_back, mixing_start, (value_rows, documents, blended_slope.reshape(row_count, SEQ, D))
    )
    value_slope = value_slopes.reshape(row_count * SEQ, D)
    value_grad = contract_rows(normed_low, value_slope)
    normed_slope = times_transpose(value_slope, value_full)
    back_first, gain_first_sum, shift_first_sum = norm_back(
        normed_slope, unit_first, recip_first, gain_first
    )
    inputs_slope = (middle_slope + back_first).astype(jnp.bfloat16)
    sums_half = (
        lax.psum_scatter(
            hidden_grad.astype(jnp.bfloat16), "wide", scatter_dimension=1, tiled=True
        ).astype(jnp.float32),
        lax.psum_scatter(
            down_grad.astype(jnp.bfloat16), "wide", scatter_dimension=0, tiled=True
        ).astype(jnp.float32),
    )
    hidden_share, down_share = (
        lax.psum_scatter(
            sums_half[0].astype(jnp.bfloat16), "narrow", scatter_dimension=0, tiled=True
        ).astype(jnp.float32),
        lax.psum_scatter(
            sums_half[1].astype(jnp.bfloat16), "narrow", scatter_dimension=1, tiled=True
        ).astype(jnp.float32),
    )
    shares = (
        lax.psum_scatter(
            mixing_grad.astype(jnp.bfloat16), "narrow", scatter_dimension=1, tiled=True
        ).astype(jnp.float32),
        lax.psum_scatter(
            value_grad.astype(jnp.bfloat16), "narrow", scatter_dimension=1, tiled=True
        ).astype(jnp.float32),
        lax.psum_scatter(
            output_grad.astype(jnp.bfloat16), "narrow", scatter_dimension=0, tiled=True
        ).astype(jnp.float32),
        lax.psum_scatter(
            gain_first_sum.astype(jnp.bfloat16), "narrow", scatter_dimension=0, tiled=True
        ).astype(jnp.float32),
        lax.psum_scatter(
            shift_first_sum.astype(jnp.bfloat16), "narrow", scatter_dimension=0, tiled=True
        ).astype(jnp.float32),
        lax.psum_scatter(
            gain_second_sum.astype(jnp.bfloat16), "narrow", scatter_dimension=0, tiled=True
        ).astype(jnp.float32),
        lax.psum_scatter(
            shift_second_sum.astype(jnp.bfloat16), "narrow", scatter_dimension=0, tiled=True
        ).astype(jnp.float32),
        lax.psum_scatter(
            hidden_bias_sum.astype(jnp.bfloat16), "narrow", scatter_dimension=0, tiled=True
        ).astype(jnp.float32),
        lax.psum_scatter(
            down_bias_sum.astype(jnp.bfloat16), "narrow", scatter_dimension=0, tiled=True
        ).astype(jnp.float32),
    )
    totals = (
        lax.psum(shares[0].astype(jnp.bfloat16), "wide").astype(jnp.float32),
        lax.psum(shares[1].astype(jnp.bfloat16), "wide").astype(jnp.float32),
        lax.psum(shares[2].astype(jnp.bfloat16), "wide").astype(jnp.float32),
        lax.psum(shares[3].astype(jnp.bfloat16), "wide").astype(jnp.float32),
        lax.psum(shares[4].astype(jnp.bfloat16), "wide").astype(jnp.float32),
        lax.psum(shares[5].astype(jnp.bfloat16), "wide").astype(jnp.float32),
        lax.psum(shares[6].astype(jnp.bfloat16), "wide").astype(jnp.float32),
        lax.psum(shares[7].astype(jnp.bfloat16), "wide").astype(jnp.float32),
        lax.psum(shares[8].astype(jnp.bfloat16), "wide").astype(jnp.float32),
    )
    return (
        result.reshape(row_count, SEQ, D).astype(jnp.bfloat16),
        inputs_slope.reshape(row_count, SEQ, D),
        totals[0],
        totals[1],
        totals[2],
        totals[3],
        totals[4],
        totals[5],
        totals[6],
        hidden_share,
        totals[7],
        down_share,
        totals[8],
    )


def solution(mesh):
    return jax.shard_map(
        local,
        mesh=mesh,
        in_specs=(
            P(("narrow", "wide"), None, None),
            P(("narrow", "wide"), None),
            P(None, "narrow", None),
            P(None, "narrow"),
            P("narrow", None),
            P("narrow"),
            P("narrow"),
            P("narrow"),
            P("narrow"),
            P("narrow", "wide"),
            P("narrow"),
            P("wide", "narrow"),
            P("narrow"),
            P(("narrow", "wide"), None, None),
        ),
        out_specs=(
            P(("narrow", "wide"), None, None),
            P(("narrow", "wide"), None, None),
            P(None, "narrow", None),
            P(None, "narrow"),
            P("narrow", None),
            P("narrow"),
            P("narrow"),
            P("narrow"),
            P("narrow"),
            P("narrow", "wide"),
            P("narrow"),
            P("wide", "narrow"),
            P("narrow"),
        ),
        check_vma=False,
    )
```

profile of v0, /device:TPU:0, one launch (start us, length us, event | category | flops | bytes accessed | tf_op | source)
XLA Modules:
  0.0 763.4 jit_solution(236922017858329842)
XLA Ops:
  8.0 4.6 copy.48
  35.7 4.7 all-gather.14.cloned.1.call-done
  40.4 8.6 %copy.50 = bf16[12,512,512]{2,1,0:T(8,128)(2,1)} copy(bf16[12,512,512]{1,2,0:T(8,128)(2,1)} %all-gather.14.cloned.1.call-done) | data formatting | bytes 12582912 | tf_op jit(solution)/shard_map/while | solution.py:116
  49.1 30.7 %while.23 = (s32[]{:T(128)}, bf16[2,512,768]{2,1,0:T(8,128)(2,1)}, bf16[2,512,768]{1,2,0:T(8,128)(2,1)S(1)}, s32[2,512]{1,0:T(2,128)S(1)}, bf16[12,512,512]{2,1,0:T(8,128)(2,1)}, /*index=5*/s32[]{:T(128)}) while((s32[]{:T(128)}, bf16[2,512,768]{2,1,0:T(8,128)(2,1)}, bf16[2,512,768]{1,2,0:T(8,128)(2,1)S(1)}, s32[2,512]{1,0:T(2,128)S(1)}, ...), condition=%wide.region_5.6_spmd, body=%wide.region_2.5_spmd.sunk | while | flops 428474880 | bytes 38328408 | solution.py:116
  49.4 11.1 %fusion.103 = (f32[12,512]{1,0:T(8,128)S(1)}, f32[12,512,512]{2,1,0:T(8,128)S(1)}) fusion(bf16[12,512,512]{2,1,0:T(8,128)(2,1)} %get-tuple-element.308, pred[512,512]{1,0:T(8,128)(4,1)S(1)} %broadcast_compare_fusion.4), kind=kOutput, calls=%fused_computation.106.clone.1 | output fusion | flops 18874880 | bytes 19161088 | tf_op jit(solution)/shard_map/while/body/eval_jaxpr/sub | solution.py:52
  64.8 10.9 %fusion.103 = (f32[12,512]{1,0:T(8,128)S(1)}, f32[12,512,512]{2,1,0:T(8,128)S(1)}) fusion(bf16[12,512,512]{2,1,0:T(8,128)(2,1)} %get-tuple-element.308, pred[512,512]{1,0:T(8,128)(4,1)S(1)} %broadcast_compare_fusion.4), kind=kOutput, calls=%fused_computation.106.clone.1 | output fusion | flops 18874880 | bytes 19161088 | tf_op jit(solution)/shard_map/while/body/eval_jaxpr/sub | solution.py:52
  85.8 51.0 %all-gather.18.cloned.1.call-done = bf16[768,3072]{0,1:T(8,128)(2,1)} async-done(((bf16[768,192]{0,1:T(8,128)(2,1)}), bf16[768,3072]{0,1:T(8,128)(2,1)}) %all-gather.18.cloned.1.call-update) | async-done | bytes 4718608 | tf_op jit(solution)/shard_map/all_gather | solution.py:95
  136.8 8.2 %fusion.62 = f32[1024,3072]{1,0:T(8,128)S(1)} fusion(bf16[768,3072]{0,1:T(8,128)(2,1)} %all-gather.18.cloned.1.call-done, f32[1024,768]{1,0:T(8,128)} %copy-done.2, f32[768]{0:T(1024)S(1)} %reshape.259, f32[768]{0:T(1024)S(1)} %reshape.258, f32[1024]{0:T(1024)S(1)} %add_rsqrt_fusion, f32[1024]{0:T(1024)S(1)} %broadcast_multiply_fusion.4), kind=kOutput, calls=%fused_computation.105 | convolution fusion | flops 4835770368 | bytes 20461568 | tf_op jit(solution)/shard_map/dot_general | solution.py:120
  144.9 4.6 copy-done.37
  149.5 9.8 %convolution_convert_fusion = bf16[3072,768]{1,0:T(8,128)(2,1)} fusion(bf16[1024,768]{1,0:T(8,128)(2,1)S(1)} %bitcast.119, f32[1024,3072]{1,0:T(8,128)S(1)} %fusion.62, f32[3072]{0:T(1024)S(1)} %bitcast.136), kind=kOutput, calls=%fused_computation.46 | convolution fusion | flops 4865654784 | bytes 18886656 | tf_op jit(solution)/shard_map/dot_general | solution.py:37
  159.3 59.2 %all-gather.20.cloned.1.call-done = bf16[3072,768]{1,0:T(8,128)(2,1)} async-done(((bf16[192,768]{1,0:T(8,128)(2,1)}), bf16[3072,768]{1,0:T(8,128)(2,1)}) %all-gather.20.cloned.1.call-update) | async-done | bytes 4718608 | tf_op jit(solution)/shard_map/all_gather | solution.py:96
  218.5 15.5 %fusion.65 = (bf16[3072]{0:T(1024)(128)(2,1)}, bf16[1024,3072]{1,0:T(8,128)(2,1)S(1)}) fusion(f32[1024,3072]{1,0:T(8,128)} %copy-done.37, f32[3072]{0:T(1024)S(1)} %bitcast.137, bf16[1024,768]{1,0:T(8,128)(2,1)S(1)} %bitcast.120, bf16[3072,768]{1,0:T(8,128)(2,1)} %all-gather.20.cloned.1.call-done), kind=kOutput, calls=%fused_computation.108 | convolution fusion | flops 4901041152 | bytes 25184256 | tf_op jit(solution)/shard_map/dot_general | solution.py:43
  234.0 10.2 %multiply_reduce_fusion.1 = (bf16[768]{0:T(1024)(128)(2,1)}, f32[1024]{0:T(1024)S(1)}, f32[1024]{0:T(1024)S(1)}, bf16[768]{0:T(1024)(128)(2,1)}, f32[1024,768]{1,0:T(8,128)}) fusion(f32[1024,768]{1,0:T(8,128)S(1)} %copy-done.3, f32[1024]{0:T(1024)S(1)} %add_rsqrt_fusion, f32[1024]{0:T(1024)S(1)} %broadcast_multiply_fusion.4, f32[768]{0:T(1024)S(1)} %reshape.258, ...), kind=kOutput, calls=%fused_computation.71 | convolution fusion | flops 4838912000 | bytes 17324032 | tf_op jit(solution)/shard_map/dot_general | solution.py:43
  244.2 7.7 %convolution_convert_fusion.1 = bf16[768,3072]{0,1:T(8,128)(2,1)} fusion(bf16[1024,3072]{1,0:T(8,128)(2,1)S(1)} %get-tuple-element.203, f32[1024,768]{1,0:T(8,128)S(1)} %copy-done.3, f32[768]{0:T(1024)S(1)} %reshape.259, f32[768]{0:T(1024)S(1)} %reshape.258, f32[1024]{0:T(1024)S(1)} %add_rsqrt_fusion, f32[1024]{0:T(1024)S(1)} %broadcast_multiply_fusion.4), kind=kOutput, calls=%fused_computation.47 | convolution fusion | flops 4838129664 | bytes 14170112 | tf_op jit(solution)/shard_map/dot_general | solution.py:37
  258.3 111.3 %while.24 = (s32[]{:T(128)}, f32[12,512,512]{1,2,0:T(8,128)}, bf16[2,512,768]{1,2,0:T(8,128)(2,1)}, s32[2,512]{1,0:T(2,128)S(1)}, bf16[12,512,512]{1,2,0:T(8,128...) while((s32[]{:T(128)}, f32[12,512,512]{1,2,0:T(8,128)}, ...), condition=%wide.region_14.15_spmd.clone, body=%wide.region_10.14_spmd.clone.sunk | while | flops 1290417664 | bytes 79771768 | solution.py:162
  260.2 14.9 %fusion.113 = (f32[12,512]{1,0:T(8,128)S(1)}, f32[12,512,512]{1,2,0:T(8,128)}) fusion(bf16[12,512,512]{1,2,0:T(8,128)(2,1)} %get-tuple-element.332, pred[512,512]{0,1:T(8,128)(4,1)S(1)} %broadcast_compare_fusion.5), kind=kOutput, calls=%fused_computation.23.clone.1 | output fusion | flops 18874880 | bytes 19161088 | tf_op jit(solution)/shard_map/while/body/eval_jaxpr/sub | solution.py:52
  275.1 10.9 %fusion.114 = bf16[12,64,512]{2,1,0:T(8,128)(2,1)} fusion(bf16[512,12,64]{0,2,1:T(8,128)(2,1)S(1)} %bitcast.112, bf16[12,512,512]{1,2,0:T(8,128)(2,1)} %get-tuple-element.332, f32[12,512]{1,0:T(8,128)S(1)} %get-tuple-element.288, pred[512,512]{0,1:T(8,128)(4,1)S(1)} %broadcast_compare_fusion.5), kind=kOutput, calls=%fused_computation.29.clone.1 | convolution fusion | flops 425073152 | bytes 8151040 | tf_op jit(solution)/shard_map/while/body/eval_jaxpr/hij,ihd->jhd/dot_general | solution.py:153
  288.1 24.2 %select_add_fusion.2 = f32[12,512,512]{1,2,0:T(8,128)} fusion(f32[12,512,512]{1,2,0:T(8,128)} %get-tuple-element.320, pred[]{:T(512)S(6)} %compare.3, bf16[512,12,64]{0,2,1:T(8,128)(2,1)S(1)} %bitcast.113, bf16[512,12,64]{0,2,1:T(8,128)(2,1)S(1)} %bitcast.116, f32[12,512]{1,0:T(8,128)S(1)} %get-tuple-element.288, ...), kind=kOutput, calls=%fused_computation.16.clone.1 | convolution fusion | flops 846207488 | bytes 45899776 | tf_op jit(solution)/shard_map/while/body/eval_jaxpr/sub | solution.py:151
  314.1 14.9 %fusion.113 = (f32[12,512]{1,0:T(8,128)S(1)}, f32[12,512,512]{1,2,0:T(8,128)}) fusion(bf16[12,512,512]{1,2,0:T(8,128)(2,1)} %get-tuple-element.332, pred[512,512]{0,1:T(8,128)(4,1)S(1)} %broadcast_compare_fusion.5), kind=kOutput, calls=%fused_computation.23.clone.1 | output fusion | flops 18874880 | bytes 19161088 | tf_op jit(solution)/shard_map/while/body/eval_jaxpr/sub | solution.py:52
  329.0 10.9 %fusion.114 = bf16[12,64,512]{2,1,0:T(8,128)(2,1)} fusion(bf16[512,12,64]{0,2,1:T(8,128)(2,1)S(1)} %bitcast.112, bf16[12,512,512]{1,2,0:T(8,128)(2,1)} %get-tuple-element.332, f32[12,512]{1,0:T(8,128)S(1)} %get-tuple-element.288, pred[512,512]{0,1:T(8,128)(4,1)S(1)} %broadcast_compare_fusion.5), kind=kOutput, calls=%fused_computation.29.clone.1 | convolution fusion | flops 425073152 | bytes 8151040 | tf_op jit(solution)/shard_map/while/body/eval_jaxpr/hij,ihd->jhd/dot_general | solution.py:153
  342.0 27.5 %select_add_fusion.2 = f32[12,512,512]{1,2,0:T(8,128)} fusion(f32[12,512,512]{1,2,0:T(8,128)} %get-tuple-element.320, pred[]{:T(512)S(6)} %compare.3, bf16[512,12,64]{0,2,1:T(8,128)(2,1)S(1)} %bitcast.113, bf16[512,12,64]{0,2,1:T(8,128)(2,1)S(1)} %bitcast.116, f32[12,512]{1,0:T(8,128)S(1)} %get-tuple-element.288, ...), kind=kOutput, calls=%fused_computation.16.clone.1 | convolution fusion | flops 846207488 | bytes 45899776 | tf_op jit(solution)/shard_map/while/body/eval_jaxpr/sub | solution.py:151
  375.0 4.3 convolution_convert_fusion.4
  379.4 10.1 %copy.55 = bf16[12,512,512]{2,1,0:T(8,128)(2,1)} copy(f32[12,512,512]{1,2,0:T(8,128)} %get-tuple-element.80) | data formatting | bytes 18874368 | tf_op jit(solution)/shard_map/while | solution.py:162
  391.6 110.5 %reduce-scatter.18.cloned.1.call-done = bf16[768,192]{0,1:T(8,128)(2,1)} async-done(((bf16[768,3072]{0,1:T(8,128)(2,1)}), bf16[768,192]{0,1:T(8,128)(2,1)}) %reduce-scatter.18.cloned.1.call-update) | async-done | bytes 294928 | tf_op jit(solution)/shard_map/reduce_scatter | solution.py:173
  504.0 8.5 %reduce-scatter.22.cloned.1.call-done = bf16[384,768]{1,0:T(8,128)(2,1)} async-done(((bf16[768,768]{1,0:T(8,128)(2,1)}), bf16[384,768]{1,0:T(8,128)(2,1)}) %reduce-scatter.22.cloned.1.call-update) | async-done | bytes 589840
  514.7 10.7 %reduce-scatter.16.cloned.1.call-done = bf16[384,768]{1,0:T(8,128)(2,1)} async-done(((bf16[768,768]{1,0:T(8,128)(2,1)}), bf16[384,768]{1,0:T(8,128)(2,1)}) %reduce-scatter.16.cloned.1.call-update) | async-done | bytes 589840 | tf_op jit(solution)/shard_map/reduce_scatter | solution.py:195
  525.3 18.5 %reduce-scatter.14.cloned.1.call-done = bf16[12,256,512]{2,1,0:T(8,128)(2,1)} async-done(((bf16[12,512,512]{2,1,0:T(8,128)(2,1)}), bf16[12,256,512]{2,1,0:T(8,128)(2,1)}) %reduce-scatter.14.cloned.1.call-update) | async-done | bytes 3145744 | tf_op jit(solution)/shard_map/reduce_scatter | solution.py:189
  549.7 4.6 fusion.52
  558.1 44.8 %all-reduce.6 = (bf16[384]{0:T(512)(128)(2,1)S(1)}, bf16[384]{0:T(512)(128)(2,1)S(1)}, bf16[384]{0:T(512)(128)(2,1)S(1)}, bf16[384]{0:T(512)(128)(2,1)S(1)}, bf1...) all-reduce(bf16[384]{0:T(512)(128)(2,1)S(1)} %dynamic-slice.1, ...), channel_id=1, replica_groups=mesh['narrow'=2,'wide'=16] {'wide'}, use_global_device_ids=true, to_apply=%region_25.26 | all-reduce | flops 3456 | bytes 13824 | tf_op jit(solution)/shard_map/psum | solution.py:221
  606.5 4.8 fusion.51
  611.3 13.1 %add_convert_fusion = bf16[1024,768]{1,0:T(8,128)(2,1)} fusion(f32[1024,768]{1,0:T(8,128)S(1)} %copy-done.4, bf16[3072,768]{1,0:T(8,128)(2,1)} %all-gather.20.cloned.1.call-done, f32[768]{0:T(1024)S(1)} %reshape.261, f32[1024,3072]{1,0:T(8,128)} %copy-done.37, f32[3072]{0:T(1024)S(1)} %bitcast.138), kind=kOutput, calls=%fused_computation.74 | convolution fusion | flops 4865654784 | bytes 22035456 | tf_op jit(solution)/shard_map/dot_general | solution.py:123
  628.0 120.6 %all-reduce.11.cloned.1.call-done = (bf16[12,256,512]{2,1,0:T(8,128)(2,1)}, bf16[768,384]{1,0:T(8,128)(2,1)}, bf16[384,768]{1,0:T(8,128)(2,1)}) async-done(((bf16[12,256,512]{2,1,0:T(8,128)(2,1)}, bf16[768,384]{1,0:T(8,128)(2,1)}, bf16[384,768]{1,0:T(8,128)(2,1)}), (bf16[12,256,512]{2,1,0:T(8,128)(2,1)}, bf16[768,384]{1,0:T(8,128)(2,1)}, bf16[384,768]{1,0:T(8,128)(2,1)})) %all-reduce.11.cloned.1.call-update) | async-done | bytes 4325392 | tf_op jit(solution)/shard_map/psum | solution.py:218
  (202 shorter events, 87.1 us)
Async XLA Ops:
  7.2 22.4 %all-gather.12.cloned.1.call-start = ((), (), s32[]{:S(2)}) async-start(), calls=%async_computation.7 | async-start | bytes 1769472 | tf_op jit(solution)/shard_map/all_gather | solution.py:74
  7.9 32.5 %all-gather.14.cloned.1.call-start = ((), (), s32[]{:S(2)}) async-start(), calls=%async_computation.8 | async-start | bytes 9437184 | tf_op jit(solution)/shard_map/all_gather | solution.py:73
  12.6 7.3 copy-start.30
  12.6 9.2 %copy-start.31 = (bf16[384]{0:T(512)(128)(2,1)S(1)}, bf16[384]{0:T(512)(128)(2,1)}, u32[]{:S(2)}) copy-start(bf16[384]{0:T(512)(128)(2,1)} %param.25) | copy-start | bytes 2308
  12.6 11.0 %copy-start.32 = (bf16[384]{0:T(512)(128)(2,1)S(1)}, bf16[384]{0:T(512)(128)(2,1)}, u32[]{:S(2)}) copy-start(bf16[384]{0:T(512)(128)(2,1)} %param.26) | copy-start | bytes 2308
  12.6 12.8 %copy-start = (bf16[2,512,768]{2,1,0:T(8,128)(2,1)S(1)}, bf16[2,512,768]{2,1,0:T(8,128)(2,1)}, u32[]{:S(2)}) copy-start(bf16[2,512,768]{2,1,0:T(8,128)(2,1)} %param.18) | copy-start | bytes 4718596
  12.7 14.4 %copy-start.26 = (bf16[1536]{0:T(1024)(128)(2,1)S(1)}, bf16[1536]{0:T(1024)(128)(2,1)}, u32[]{:S(2)}) copy-start(bf16[1536]{0:T(1024)(128)(2,1)} %param.28) | copy-start | bytes 9220
  12.7 67.1 %all-gather.16.cloned.1.call-start = ((), (), s32[]{:S(2)}) async-start(), calls=%async_computation.9 | async-start | bytes 1769472 | tf_op jit(solution)/shard_map/all_gather | solution.py:75
  13.4 123.4 %all-gather.18.cloned.1.call-start = ((), (), s32[]{:S(2)}) async-start(), calls=%async_computation.10 | async-start | bytes 5013504 | tf_op jit(solution)/shard_map/all_gather | solution.py:95
  15.8 202.8 %all-gather.20.cloned.1.call-start = ((), (), s32[]{:S(2)}) async-start(), calls=%async_computation.11 | async-start | bytes 5013504 | tf_op jit(solution)/shard_map/all_gather | solution.py:96
  18.0 371.6 %reduce-scatter.20.cloned.1.call-start = ((), (), s32[]{:S(2)}) async-start(), calls=%async_computation.15 | async-start | bytes 5013504 | tf_op jit(solution)/shard_map/reduce_scatter | solution.py:176
  20.0 9.6 %copy-start.12 = (f32[768]{0:T(1024)}, f32[768]{0:T(1024)S(1)}, u32[]{:S(2)}) copy-start(f32[768]{0:T(1024)S(1)} %reshape.256) | copy-start | bytes 9220
  21.8 7.8 %copy-start.20 = (f32[768]{0:T(1024)}, f32[768]{0:T(1024)S(1)}, u32[]{:S(2)}) copy-start(f32[768]{0:T(1024)S(1)} %reshape.257) | copy-start | bytes 9220
  28.9 189.7 %copy-start.22 = (f32[2,1,1536]{2,1,0:T(1,128)}, f32[2,1,1536]{2,1,0:T(1,128)S(1)}, u32[]{:S(2)}) copy-start(f32[2,1,1536]{2,1,0:T(1,128)S(1)} %convert_element_type.240) | copy-start | bytes 36868
  35.7 13.4 %copy-start.11 = (s32[2,512]{1,0:T(2,128)S(1)}, s32[2,512]{1,0:T(2,128)}, u32[]{:S(2)}) copy-start(s32[2,512]{1,0:T(2,128)} %param.19) | copy-start | bytes 12292
  85.8 63.7 %copy-start.6 = (bf16[2,512,768]{2,1,0:T(8,128)(2,1)S(1)}, bf16[2,512,768]{2,1,0:T(8,128)(2,1)}, u32[]{:S(2)}) copy-start(bf16[2,512,768]{2,1,0:T(8,128)(2,1)} %param.31) | copy-start | bytes 4718596
  159.3 342.8 %reduce-scatter.18.cloned.1.call-start = ((), (), s32[]{:S(2)}) async-start(), calls=%async_computation.14 | async-start | bytes 5013504 | tf_op jit(solution)/shard_map/reduce_scatter | solution.py:173
  218.5 15.5 %copy-start.3 = (f32[1024,768]{1,0:T(8,128)S(1)}, f32[1024,768]{1,0:T(8,128)}, u32[]{:S(2)}) copy-start(f32[1024,768]{1,0:T(8,128)} %copy-done.2) | copy-start | bytes 9437188
  251.9 260.6 %reduce-scatter.22.cloned.1.call-start = ((), (), s32[]{:S(2)}) async-start(), calls=%async_computation.16 | async-start | bytes 1769472
  258.3 111.3 %copy-start.13 = (f32[768]{0:T(1024)S(1)}, f32[768]{0:T(1024)}, u32[]{:S(2)}) copy-start(f32[768]{0:T(1024)} %copy-done.12) | copy-start | bytes 9220
  258.3 111.4 %copy-start.19 = (f32[2,512]{1,0:T(2,128)S(1)}, f32[2,512]{1,0:T(2,128)}, u32[]{:S(2)}) copy-start(f32[2,512]{1,0:T(2,128)} %copy-done.18) | copy-start | bytes 12292
  258.3 111.4 %copy-start.21 = (f32[768]{0:T(1024)S(1)}, f32[768]{0:T(1024)}, u32[]{:S(2)}) copy-start(f32[768]{0:T(1024)} %copy-done.20) | copy-start | bytes 9220
  258.3 111.4 %copy-start.25 = (f32[2,512]{1,0:T(2,128)S(1)}, f32[2,512]{1,0:T(2,128)}, u32[]{:S(2)}) copy-start(f32[2,512]{1,0:T(2,128)} %get-tuple-element.194) | copy-start | bytes 12292
  374.9 150.4 %reduce-scatter.16.cloned.1.call-start = ((), (), s32[]{:S(2)}) async-start(), calls=%async_computation.13 | async-start | bytes 1769472 | tf_op jit(solution)/shard_map/reduce_scatter | solution.py:195
  379.3 164.5 %reduce-scatter.14.cloned.1.call-start = ((), (), s32[]{:S(2)}) async-start(), calls=%async_computation.12 | async-start | bytes 9437184 | tf_op jit(solution)/shard_map/reduce_scatter | solution.py:189
  389.5 234.8 %reduce-scatter.26.cloned.1.call-start = ((), (), s32[]{:S(2)}) async-start(), calls=%async_computation.18 | async-start | bytes 589824
  391.5 152.4 %copy-start.36 = (u32[32]{0:T(128)S(1)}, u32[32]{0:T(128)}, u32[]{:S(2)}) copy-start(u32[32]{0:T(128)} %constant.70) | copy-start | bytes 388
  391.5 234.7 %reduce-scatter.24.cloned.1.call-start = ((), (), s32[]{:S(2)}) async-start(), calls=%async_computation.17 | async-start | bytes 589824
  504.0 41.8 %copy-start.33 = (bf16[384]{0:T(512)(128)(2,1)S(1)}, bf16[384]{0:T(512)(128)(2,1)}, u32[]{:S(2)}) copy-start(bf16[384]{0:T(512)(128)(2,1)} %param.30) | copy-start | bytes 2308
  504.0 43.6 %copy-start.7 = (bf16[2,512,768]{2,1,0:T(8,128)(2,1)S(1)}, bf16[2,512,768]{2,1,0:T(8,128)(2,1)}, u32[]{:S(2)}) copy-start(bf16[2,512,768]{2,1,0:T(8,128)(2,1)} %param.31) | copy-start | bytes 4718596
  504.0 244.6 %all-reduce.11.cloned.1.call-start = ((), (), s32[]{:S(2)}) async-start(), calls=%async_computation.19 | async-start | bytes 8650752 | tf_op jit(solution)/shard_map/psum | solution.py:218
  543.8 5.8 copy-start.1
  (19 other events, 71.4 us)
Sparse Core Ops, SparseCore 0:
  9.6 11.8 all-gather.11
  23.6 16.7 all-gather.13
  42.0 10.4 all-gather.15
  55.1 81.6 all-gather.17
  139.4 79.0 all-gather.19
  223.6 136.0 reduce-scatter.19
  365.6 136.3 reduce-scatter.17
  504.9 7.6 reduce-scatter.21
  515.5 9.8 reduce-scatter.15
  528.1 15.6 reduce-scatter.13
  546.1 8.9 reduce-scatter.25
  557.2 8.9 reduce-scatter.23
  574.0 174.5 all-reduce.10
where the time goes:
time: 768 us; the launch traced here: 763 us
  waiting for transfers between devices  385 us (50%)
  matrix products  167 us (22%)
  other arithmetic  77.3 us (10%)
  blocking collectives  63.3 us (8%)
  local copies, waits for them, and re-layouts  54 us (7%)
  between operations  16.1 us (2%)
    psum x1, waiting for transfers between devices, local(): lax.psum(shares[0].astype(jnp.bfloat16), 'wide').astype(jnp.float32)  121 us
    reduce_scatter x1, waiting for transfers between devices, local(): lax.psum_scatter(hidden_grad.astype(jnp.bfloat16), 'wide', scatter_dimens...  110 us
    all_gather x1, waiting for transfers between devices, local(): lax.all_gather(halfway[1], 'wide', axis=0, tiled=True)  59.2 us
    sub x4, other arithmetic, row_chances(): raised = jnp.exp(scores - row_top)  51.8 us
    sub x2, matrix products, mix_back(): chance_slope - jnp.sum(chances * chance_slope, axis=-1, keepdims=True)  51.7 us
    all_gather x1, waiting for transfers between devices, local(): lax.all_gather(halfway[0], 'wide', axis=1, tiled=True)  51 us
    psum x1, blocking collectives, local(): lax.psum(shares[3].astype(jnp.bfloat16), 'wide').astype(jnp.float32)  44.8 us
    dot_general x4, matrix products, times_transpose(): lax.dot_general(left_side, right_side, (((1,), (1,)), ((), ())), preferre...  32.8 us
  transfers between devices with their start and end apart: 13, of which 8 were waited for; matrix products, arithmetic and copies ran while one was open for 37% of the time, Pallas kernels for 0%

commit v1 on v0

--- a/solution.py
+++ b/solution.py
@@ -1,15 +1,528 @@
+import functools
+
 import jax
 import jax.numpy as jnp
 from jax import lax
+from jax.experimental import pallas as pl
+from jax.experimental.pallas import tpu as pltpu
 from jax.sharding import PartitionSpec as P
 
 D = 768
 HEADS = 12
 HEAD = 64
 SEQ = 512
-
-
+FF = 3072
+HALF = D // 2
+CHUNK = 192
+GROUP = 4 * CHUNK
 epsilon = 1e-05
+
+MESH = pl.DeviceIdType.MESH
+f32 = jnp.float32
+bf16 = jnp.bfloat16
+
+
+def place():
+    core = lax.axis_index("narrow")
+    wide = lax.axis_index("wide")
+    return core, lax.rem(wide, 2), lax.rem(lax.div(wide, 2), 2), lax.div(wide, 4)
+
+
+def seat(core, x, y, z):
+    return (core, z * 4 + y * 2 + x)
+
+
+def remote(src, dst, send_sem, recv_sem, device):
+    return pltpu.make_async_remote_copy(
+        src_ref=src,
+        dst_ref=dst,
+        send_sem=send_sem,
+        recv_sem=recv_sem,
+        device_id=device,
+        device_id_type=MESH,
+    )
+
+
+def greet(core, x, y, z):
+    barrier = pltpu.get_barrier_semaphore()
+    for device in (seat(1 - core, x, y, z), seat(core, 1 - x, y, z), seat(core, x, 1 - y, z)):
+        pl.semaphore_signal(barrier, inc=1, device_id=device, device_id_type=MESH)
+
+    @pl.when(z < 3)
+    def _():
+        pl.semaphore_signal(
+            barrier, inc=1, device_id=seat(core, x, y, z + 1), device_id_type=MESH
+        )
+
+    @pl.when(z > 0)
+    def _():
+        pl.semaphore_signal(
+            barrier, inc=1, device_id=seat(core, x, y, z - 1), device_id_type=MESH
+        )
+
+    above, below = jnp.where(z < 3, 1, 0), jnp.where(z > 0, 1, 0)
+    pl.semaphore_wait(barrier, 3 + above + below)
+
+
+def halves(core):
+    mine = pl.ds(pl.multiple_of(core * HALF, 128), HALF)
+    other = pl.ds(pl.multiple_of((1 - core) * HALF, 128), HALF)
+    return mine, other
+
+
+def line_order(z, step):
+    table = ((0, 1, 2, 3), (1, 0, 2, 3), (2, 3, 1, 0), (3, 2, 1, 0))
+    return jnp.where(
+        z == 0,
+        table[0][step],
+        jnp.where(z == 1, table[1][step], jnp.where(z == 2, table[2][step], table[3][step])),
+    )
+
+
+def unit_of(rows):
+    center = rows - jnp.mean(rows, axis=-1, keepdims=True)
+    reciprocal = lax.rsqrt(jnp.mean(center * center, axis=-1, keepdims=True) + epsilon)
+    return center * reciprocal, reciprocal
+
+
+def dot_nn(left, right):
+    return lax.dot_general(left, right, (((1,), (0,)), ((), ())), preferred_element_type=f32)
+
+
+def dot_nt(left, right):
+    return lax.dot_general(left, right, (((1,), (1,)), ((), ())), preferred_element_type=f32)
+
+
+def dot_tn(left, right):
+    return lax.dot_general(left, right, (((0,), (0,)), ((), ())), preferred_element_type=f32)
+
+
+def lane_ids(rows):
+    return lax.broadcasted_iota(jnp.int32, (rows, 128), 1)
+
+
+def fill_mask(docs_ref, mask, rows):
+    for r in range(rows):
+        flat = docs_ref[r : r + 1, :].astype(f32)
+        for i in range(0, SEQ, 128):
+            tall = jnp.broadcast_to(flat[:, i : i + 128], (128, 128)).T
+            for j in range(0, SEQ, 128):
+                wide = jnp.broadcast_to(flat[:, j : j + 128], (128, 128))
+                mask[r, i : i + 128, j : j + 128] = jnp.where(tall == wide, 1.0, 0.0).astype(bf16)
+
+
+def forward_kernel(
+    x_ref, docs_ref, mixing_ref, value_ref, output_ref, shard_ref, vector_ref,
+    full_ref, raised_out, value_out, output_out, vector_out, normed_out, values_out, blended_out,
+    share_out, middle_out,
+    raised, value_full, output_full, mask, vector_full, normed, values, blended, share, middle,
+    recv, core_recv, sent_x, sent_y, sent_up, sent_down, sent_core,
+    early_send, early_recv, local_sem, out_sem,
+):
+    core, x, y, z = place()
+    mine, other = halves(core)
+    near_x, near_y = seat(core, 1 - x, y, z), seat(core, x, 1 - y, z)
+    above, below = seat(core, x, y, z + 1), seat(core, x, y, z - 1)
+    twin = seat(1 - core, x, y, z)
+    tokens = x_ref.shape[0]
+
+    def chunk_of(k, y_of, x_of):
+        return k * 4 + y_of * 2 + x_of
+
+    def slot(m, chunk, lanes):
+        rows = pl.ds(pl.multiple_of(chunk * CHUNK, CHUNK), CHUNK)
+        return full_ref.at[m, rows, lanes]
+
+    own = chunk_of(z, y, x)
+
+    def send(m, chunk, sems, device):
+        src = slot(m, chunk, mine)
+        return remote(src, src, sems.at[m, chunk], recv.at[m, chunk], device)
+
+    def send_own(m, sems, device):
+        return remote(shard_ref.at[m], slot(m, own, mine), sems.at[m, own], recv.at[m, own], device)
+
+    def send_twin(m, chunk):
+        src = slot(m, chunk, mine)
+        return remote(src, src, sent_core.at[m, chunk], core_recv.at[m, chunk], twin)
+
+    def arrived(m, chunk):
+        send(m, chunk, sent_x, near_x).wait_recv()
+
+    heads_part = HEADS // 4
+    my_rows = pl.ds(pl.multiple_of(core * (SEQ // 2), SEQ // 2), SEQ // 2)
+
+    def mixing_part(p):
+        heads = pl.ds(p * heads_part, heads_part)
+        return mixing_ref.at[heads], raised.at[heads, my_rows]
+
+    early = [
+        (vector_ref, vector_full.at[:, mine]),
+        (value_ref, value_full.at[:, mine]),
+        mixing_part(0), mixing_part(1), mixing_part(2), mixing_part(3),
+        (output_ref, output_full.at[mine, :]),
+    ]
+    greet(core, x, y, z)
+    early_sends = [
+        remote(src, dst, early_send.at[n], early_recv.at[n], twin)
+        for n, (src, dst) in enumerate(early)
+    ]
+    early_local = [
+        pltpu.make_async_copy(src, dst, local_sem.at[n]) for n, (src, dst) in enumerate(early)
+    ]
+    own_local = [
+        pltpu.make_async_copy(shard_ref.at[m], slot(m, own, mine), local_sem.at[7 + m])
+        for m in range(2)
+    ]
+    for m in range(2):
+        own_local[m].start()
+    send_own(0, sent_x, near_x).start()
+    send_own(1, sent_y, near_y).start()
+
+    @pl.when(z < 3)
+    def _():
+        for m in range(2):
+            send_own(m, sent_up, above).start()
+
+    @pl.when(z > 0)
+    def _():
+        for m in range(2):
+            send_own(m, sent_down, below).start()
+
+    send_own(1, sent_x, near_x).start()
+    send_own(0, sent_y, near_y).start()
+    for copy in early_sends:
+        copy.start()
+    for copy in early_local:
+        copy.start()
+    for m in range(2):
+        own_local[m].wait()
+        send_twin(m, own).start()
+
+    def early_ready(n):
+        early_local[n].wait()
+        early_sends[n].wait_recv()
+
+    def line_event(step):
+        k = line_order(z, step)
+        chunk = chunk_of(k, y, x)
+        for m in range(2):
+            arrived(m, chunk)
+
+            @pl.when(jnp.logical_and(k < z, z < 3))
+            def _():
+                send(m, chunk, sent_up, above).start()
+
+            @pl.when(jnp.logical_and(k > z, z > 0))
+            def _():
+                send(m, chunk, sent_down, below).start()
+
+            if m == 0:
+                send(0, chunk, sent_x, near_x).start()
+            else:
+                send(1, chunk, sent_y, near_y).start()
+        send(1, chunk, sent_x, near_x).start()
+        send(0, chunk, sent_y, near_y).start()
+        for m in range(2):
+            send_twin(m, chunk).start()
+
+    def cross_event(step):
+        k = line_order(z, step)
+        across_x, across_y = chunk_of(k, y, 1 - x), chunk_of(k, 1 - y, x)
+        arrived(0, across_x)
+        send(0, across_x, sent_y, near_y).start()
+        arrived(1, across_y)
+        send(1, across_y, sent_x, near_x).start()
+        send_twin(0, across_x).start()
+        send_twin(1, across_y).start()
+
+    def rest_event(step):
+        k = line_order(z, step)
+        across_x, across_y = chunk_of(k, y, 1 - x), chunk_of(k, 1 - y, x)
+        arrived(1, across_x)
+        send_twin(1, across_x).start()
+        arrived(0, across_y)
+        send_twin(0, across_y).start()
+
+    def last_event(step):
+        k = line_order(z, step)
+        corner = chunk_of(k, 1 - y, 1 - x)
+        for m in range(2):
+            arrived(m, corner)
+            send_twin(m, corner).start()
+
+    def out_copy(n, src, dst):
+        return pltpu.make_async_copy(src, dst, out_sem.at[n])
+
+    block = 256
+    early_ready(0)
+    gain, shift = vector_full[0:1, :], vector_full[1:2, :]
+    early_ready(1)
+
+    def first_norm(b, _):
+        rows = pl.ds(pl.multiple_of(b * block, block), block)
+        unit, _r = unit_of(x_ref[rows, :].astype(f32))
+        low = (unit * gain + shift).astype(bf16)
+        normed[rows, :] = low
+        values[rows, :] = dot_nn(low, value_full[...]).astype(bf16)
+        return 0
+
+    lax.fori_loop(0, tokens // block, first_norm, 0)
+    out_normed = out_copy(0, normed, normed_out)
+    out_normed.start()
+    out_values = out_copy(1, values, values_out)
+    out_values.start()
+    out_value = out_copy(2, value_full, value_out)
+    out_value.start()
+    cross_event(0)
+    fill_mask(docs_ref, mask, tokens // SEQ)
+
+    def mix_pair(p, _):
+        lanes = pl.ds(pl.multiple_of(p * 128, 128), 128)
+        left_half = lane_ids(SEQ) < HEAD
+        for i in range(0, SEQ, block):
+            for half in range(2):
+                h = 2 * p + half
+                raised[h, i : i + block] = jnp.exp(raised[h, i : i + block].astype(f32)).astype(bf16)
+        for r in range(tokens // SEQ):
+            rows = pl.ds(r * SEQ, SEQ)
+            pair = values[rows, lanes]
+            ones = jnp.ones_like(pair)
+            first = jnp.where(left_half, pair, ones)
+            second = jnp.where(left_half, ones, pair)
+            for i in range(0, SEQ, block):
+                keep = mask[r, i : i + block]
+                one = dot_nn(raised[2 * p, i : i + block] * keep, first)
+                two = dot_nn(raised[2 * p + 1, i : i + block] * keep, second)
+                low_lanes = left_half[:block]
+                part = 1.0 / pltpu.roll(jnp.where(low_lanes, two, one), HEAD, 1)
+                done = pl.ds(r * SEQ + i, block)
+                share[done, lanes] = part
+                blended[done, lanes] = (jnp.where(low_lanes, one, two) * part).astype(bf16)
+        return 0
+
+    for n in (2, 3):
+        early_ready(n)
+    lax.fori_loop(0, 3, mix_pair, 0)
+    line_event(1)
+    rest_event(0)
+    for n in (4, 5):
+        early_ready(n)
+    lax.fori_loop(3, 6, mix_pair, 0)
+    last_event(0)
+    cross_event(1)
+    outs = [
+        out_copy(3, blended, blended_out), out_copy(4, share, share_out),
+        out_copy(5, raised, raised_out), out_copy(6, vector_full, vector_out),
+    ]
+    for copy in outs:
+        copy.start()
+    early_ready(6)
+
+    def project(b, _):
+        rows = pl.ds(pl.multiple_of(b * block, block), block)
+        middle[rows, :] = x_ref[rows, :].astype(f32) + dot_nn(blended[rows, :], output_full[...])
+        return 0
+
+    lax.fori_loop(0, tokens // block, project, 0)
+    outs.append(out_copy(7, middle, middle_out))
+    outs.append(out_copy(8, output_full, output_out))
+    outs[-1].start()
+    outs[-2].start()
+    line_event(2)
+    rest_event(1)
+    last_event(1)
+    cross_event(2)
+    line_event(3)
+    rest_event(2)
+    last_event(2)
+    cross_event(3)
+    rest_event(3)
+    last_event(3)
+
+    for copy in outs + [out_normed, out_values, out_value]:
+        copy.wait()
+    for copy in early_sends:
+        copy.wait_send()
+
+    def settle(chunk, _):
+        for m in range(2):
+            copy = send_twin(m, chunk)
+            copy.wait_recv()
+            copy.wait_send()
+        return 0
+
+    lax.fori_loop(0, 16, settle, 0)
+
+    def settle_line(k, _):
+        line = chunk_of(k, y, x)
+        for m in range(2):
+            send(m, line, sent_x, near_x).wait_send()
+            send(m, line, sent_y, near_y).wait_send()
+
+            @pl.when(jnp.logical_and(k <= z, z < 3))
+            def _():
+                send(m, line, sent_up, above).wait_send()
+
+            @pl.when(jnp.logical_and(k >= z, z > 0))
+            def _():
+                send(m, line, sent_down, below).wait_send()
+
+        send(0, chunk_of(k, y, 1 - x), sent_y, near_y).wait_send()
+        send(1, chunk_of(k, 1 - y, x), sent_x, near_x).wait_send()
+        return 0
+
+    lax.fori_loop(0, 4, settle_line, 0)
+
+
+def forward_call(x, documents, mixing, value_weight, output_weight, shard, vectors):
+    tokens = x.shape[0]
+    rows = tokens // SEQ
+    any_spec = pl.BlockSpec(memory_space=pl.ANY)
+    vmem = pl.BlockSpec(memory_space=pltpu.VMEM)
+    shape = jax.ShapeDtypeStruct
+    dma = pltpu.SemaphoreType.DMA
+    return pl.pallas_call(
+        forward_kernel,
+        out_shape=(
+            shape((2, FF, D), bf16), shape((HEADS, SEQ, SEQ), bf16), shape((D, D), bf16),
+            shape((D, D), bf16), shape((16, D), f32), shape((tokens, D), bf16),
+            shape((tokens, D), bf16), shape((tokens, D), bf16), shape((tokens, D), f32),
+            shape((tokens, D), f32),
+        ),
+        in_specs=[vmem, vmem] + [any_spec] * 5,
+        out_specs=[any_spec] * 10,
+        scratch_shapes=[
+            pltpu.VMEM((HEADS, SEQ, SEQ), bf16), pltpu.VMEM((D, D), bf16), pltpu.VMEM((D, D), bf16),
+            pltpu.VMEM((rows, SEQ, SEQ), bf16), pltpu.VMEM((16, D), f32),
+            pltpu.VMEM((tokens, D), bf16), pltpu.VMEM((tokens, D), bf16),
+            pltpu.VMEM((tokens, D), bf16), pltpu.VMEM((tokens, D), f32),
+            pltpu.VMEM((tokens, D), f32),
+            dma((2, 16)), dma((2, 16)), dma((2, 16)), dma((2, 16)), dma((2, 16)), dma((2, 16)),
+            dma((2, 16)), dma((8,)), dma((8,)), dma((9,)), dma((9,)),
+        ],
+        compiler_params=pltpu.CompilerParams(
+            collective_id=0, has_side_effects=True, vmem_limit_bytes=60 << 20
+        ),
+    )(x, documents, mixing, value_weight, output_weight, shard, vectors)
+
+
+def contract_rows(left_side, right_side):
+    return dot_tn(left_side, right_side)
+
+
+def norm_back(slope_rows, unit_rows, reciprocal, norm_gain):
+    tilted = slope_rows * norm_gain
+    centered_slope = tilted - jnp.mean(tilted, axis=-1, keepdims=True)
+    centered_slope = centered_slope - unit_rows * jnp.mean(
+        tilted * unit_rows, axis=-1, keepdims=True
+    )
+    return (
+        centered_slope * reciprocal,
+        jnp.sum(slope_rows * unit_rows, axis=0),
+        jnp.sum(slope_rows, axis=0),
+    )
+
+
+def local(
+    inputs, documents, mixing, value_weight, output_weight, mixer_gain, mixer_shift, dense_gain,
+    dense_shift, hidden_weight, hidden_bias, down_weight, down_bias, cotangent,
+):
+    row_count = inputs.shape[0]
+    tokens = row_count * SEQ
+    shard = jnp.stack([hidden_weight.T, down_weight])
+    small = jnp.stack([mixer_gain, mixer_shift, dense_gain, dense_shift, down_bias])
+    vectors = jnp.concatenate(
+        [small, hidden_bias.reshape(4, HALF), jnp.zeros((7, HALF), bf16)]
+    ).astype(f32)
+    (
+        full, raised, value_full, output_full, vector_full, normed_low, values, blended, share, middle,
+    ) = forward_call(
+        inputs.reshape(tokens, D), documents, mixing, value_weight, output_weight, shard, vectors
+    )
+    gain_first, shift_first, gain_second, shift_second, bias_down = (vector_full[n] for n in range(5))
+    bias_hidden = vector_full[5:9].reshape(4, 2, HALF).swapaxes(0, 1).reshape(FF)
+    hidden_t, down_full = full[0], full[1]
+    stream = inputs.reshape(tokens, D).astype(f32)
+    unit_first, recip_first = unit_of(stream)
+    unit_second, recip_second = unit_of(middle)
+    normed_two_low = (unit_second * gain_second + shift_second).astype(bf16)
+    hidden = dot_nt(normed_two_low, hidden_t) + bias_hidden
+    activated, gelu_pull = jax.vjp(jax.nn.gelu, hidden)
+    active = activated.astype(jnp.bfloat16)
+    result = middle + dot_nn(active, down_full) + bias_down
+    slope_low = cotangent.reshape(tokens, D)
+    slope_wide = slope_low.astype(jnp.float32)
+    down_bias_sum = jnp.sum(slope_wide, axis=0)
+    down_grad = contract_rows(active, slope_low)
+    active_slope = dot_nt(slope_low, down_full)
+    hidden_slope = gelu_pull(active_slope)[0].astype(bf16)
+    hidden_bias_sum = jnp.sum(hidden_slope.astype(jnp.float32), axis=0)
+    hidden_grad = contract_rows(normed_two_low, hidden_slope)
+    normed_two_slope = dot_nn(hidden_slope, hidden_t)
+    back_second, gain_second_sum, shift_second_sum = norm_back(
+        normed_two_slope, unit_second, recip_second, gain_second
+    )
+    middle_slope = slope_wide + back_second
+    attended_slope = middle_slope.astype(jnp.bfloat16)
+    output_grad = contract_rows(blended, attended_slope)
+    blended_slope = dot_nt(attended_slope, output_full).astype(jnp.bfloat16)
+    value_rows = values.reshape(row_count, SEQ, D)
+
+    def mix_back(running, bundle):
+        row_values, row_docs, row_slope = bundle
+        same = row_docs[:, None] == row_docs[None, :]
+        chances = jnp.where(same[None], raised.astype(f32), 0.0)
+        chances = chances / jnp.sum(chances, axis=-1, keepdims=True)
+        per_head = row_values.reshape(SEQ, HEADS, HEAD)
+        head_slope = row_slope.reshape(SEQ, HEADS, HEAD)
+        chance_slope = jnp.einsum(
+            "ihd,jhd->hij", head_slope, per_head, preferred_element_type=jnp.float32
+        )
+        score_slope = chances * (
+            chance_slope - jnp.sum(chances * chance_slope, axis=-1, keepdims=True)
+        )
+        value_part = jnp.einsum(
+            "hij,ihd->jhd",
+            chances.astype(jnp.bfloat16),
+            head_slope,
+            preferred_element_type=jnp.float32,
+        )
+        return (running + score_slope, value_part.reshape(SEQ, D).astype(jnp.bfloat16))
+
+    mixing_start = jnp.zeros((HEADS, SEQ, SEQ), jnp.float32)
+    mixing_grad, value_slopes = lax.scan(
+        mix_back, mixing_start, (value_rows, documents, blended_slope.reshape(row_count, SEQ, D))
+    )
+    value_slope = value_slopes.reshape(tokens, D)
+    value_grad = contract_rows(normed_low, value_slope)
+    normed_slope = dot_nt(value_slope, value_full)
+    back_first, gain_first_sum, shift_first_sum = norm_back(
+        normed_slope, unit_first, recip_first, gain_first
+    )
+    inputs_slope = (middle_slope + back_first).astype(jnp.bfloat16)
+
+    def scatter(array, axis_name, axis):
+        return lax.psum_scatter(
+            array.astype(bf16), axis_name, scatter_dimension=axis, tiled=True
+        ).astype(f32)
+
+    hidden_share = scatter(scatter(hidden_grad, "wide", 1), "narrow", 0)
+    down_share = scatter(scatter(down_grad, "wide", 0), "narrow", 1)
+    sums = (
+        (mixing_grad, 1), (value_grad, 1), (output_grad, 0), (gain_first_sum, 0),
+        (shift_first_sum, 0), (gain_second_sum, 0), (shift_second_sum, 0), (hidden_bias_sum, 0),
+        (down_bias_sum, 0),
+    )
+    totals = [
+        lax.psum(scatter(one, "narrow", axis).astype(bf16), "wide").astype(f32)
+        for one, axis in sums
+    ]
+    return (
+        result.reshape(row_count, SEQ, D).astype(jnp.bfloat16),
+        inputs_slope.reshape(row_count, SEQ, D),
+        *totals[:7], hidden_share, totals[7], down_share, totals[8],
+    )
 
 
 def normalize(matrix, norm_gain, norm_shift):
@@ -20,7 +533,7 @@
     return (unit_rows * norm_gain + norm_shift, unit_rows, reciprocal)
 
 
-def norm_back(slope_rows, unit_rows, reciprocal, norm_gain):
+def plain_norm_back(slope_rows, unit_rows, reciprocal, norm_gain):
     tilted = slope_rows * norm_gain
     centered_slope = tilted - jnp.mean(tilted, axis=-1, keepdims=True)
     centered_slope = centered_slope - unit_rows * jnp.mean(
@@ -33,7 +546,7 @@
     )
 
 
-def contract_rows(left_side, right_side):
+def plain_contract(left_side, right_side):
     return lax.dot_general(
         left_side, right_side, (((0,), (0,)), ((), ())), preferred_element_type=jnp.float32
     )
@@ -53,7 +566,7 @@
     return raised / jnp.sum(raised, axis=-1, keepdims=True)
 
 
-def local(
+def plain(
     inputs,
     documents,
     mixing,
@@ -124,19 +637,19 @@
     slope_low = cotangent.reshape(row_count * SEQ, D)
     slope_wide = slope_low.astype(jnp.float32)
     down_bias_sum = jnp.sum(slope_wide, axis=0)
-    down_grad = contract_rows(active, slope_low)
+    down_grad = plain_contract(active, slope_low)
     active_slope = times_transpose(slope_low, down_full)
     hidden_slope_wide = gelu_pull(active_slope)[0]
     hidden_slope = hidden_slope_wide.astype(jnp.bfloat16)
     hidden_bias_sum = jnp.sum(hidden_slope.astype(jnp.float32), axis=0)
-    hidden_grad = contract_rows(normed_two_low, hidden_slope)
+    hidden_grad = plain_contract(normed_two_low, hidden_slope)
     normed_two_slope = times_transpose(hidden_slope, hidden_full)
-    back_second, gain_second_sum, shift_second_sum = norm_back(
+    back_second, gain_second_sum, shift_second_sum = plain_norm_back(
         normed_two_slope, unit_second, recip_second, gain_second
     )
     middle_slope = slope_wide + back_second
     attended_slope = middle_slope.astype(jnp.bfloat16)
-    output_grad = contract_rows(blended, attended_slope)
+    output_grad = plain_contract(blended, attended_slope)
     blended_slope = times_transpose(attended_slope, output_full).astype(jnp.bfloat16)
 
     def mix_back(running, bundle):
@@ -163,9 +676,9 @@
         mix_back, mixing_start, (value_rows, documents, blended_slope.reshape(row_count, SEQ, D))
     )
     value_slope = value_slopes.reshape(row_count * SEQ, D)
-    value_grad = contract_rows(normed_low, value_slope)
+    value_grad = plain_contract(normed_low, value_slope)
     normed_slope = times_transpose(value_slope, value_full)
-    back_first, gain_first_sum, shift_first_sum = norm_back(
+    back_first, gain_first_sum, shift_first_sum = plain_norm_back(
         normed_slope, unit_first, recip_first, gain_first
     )
     inputs_slope = (middle_slope + back_first).astype(jnp.bfloat16)
@@ -243,8 +756,9 @@
 
 
 def solution(mesh):
+    inner = local if dict(mesh.shape) == {"narrow": 2, "wide": 16} else plain
     return jax.shard_map(
-        local,
+        inner,
         mesh=mesh,
         in_specs=(
             P(("narrow", "wide"), None, None),

time: 768 us -> 649 us (0.85)
  waiting for transfers between devices: 385 us -> 304 us
  Pallas kernels: 0 us -> 58.9 us
  matrix products: 167 us -> 123 us
  other arithmetic: 77.3 us -> 36 us
  blocking collectives: 63.3 us -> 47.2 us
    all_gather x5 -> x0, waiting for transfers between devices: 115 us -> none  [the longest x1 59.2 us: local(): lax.all_gather(halfway[1], 'wide', axis=0, tiled=True)]
    pallas_call x0 -> x1, Pallas kernels: none -> 58.9 us  [forward_call(): pl.pallas_call(forward_kernel, out_shape=(shape((2, FF, D), bf16), shape(...]
    sub x4 -> x0, other arithmetic: 51.8 us -> none  [row_chances(): raised = jnp.exp(scores - row_top)]
    reduce_scatter x4, waiting for transfers between devices: 140 us -> 171 us  [scatter(): lax.psum_scatter(array.astype(bf16), axis_name, scatter_dimension=axis, t...]
    sub x2, matrix products: 51.7 us -> 33.7 us  [mix_back(): chance_slope - jnp.sum(chances * chance_slope, axis=-1, keepdims=True)]
    all_gather x8 -> x0, blocking collectives: 15.1 us -> none  [the longest x1 2.23 us: local(): lax.all_gather(hidden_weight, 'narrow', axis=0, tiled=True)]
    dot_general x14 -> x10, matrix products: 93 us -> 79.4 us  [the longest x4 30.3 us: dot_nt(): lax.dot_general(left, right, (((1,), (1,)), ((), ())), preferred_element_...]
    dot_general x2, matrix products: 21.8 us -> 10.3 us  [mix_back(): jnp.einsum('hij,ihd->jhd', chances.astype(jnp.bfloat16), head_slope, pref...]
  transfers between devices with their start and end apart: 13 -> 8, of which waited for: 8 -> 6; matrix products, arithmetic and copies ran while one was open for 37% -> 26% of each run, Pallas kernels for 0% -> 0%
where the time goes in v1:
time: 649 us; the launch traced here: 640 us
  waiting for transfers between devices  304 us (47%)
  matrix products  123 us (19%)
  Pallas kernels  58.9 us (9%)
  local copies, waits for them, and re-layouts  53.4 us (8%)
  blocking collectives  47.2 us (7%)
  other arithmetic  36 us (6%)
  between operations  16.3 us (3%)
    reduce_scatter x4, waiting for transfers between devices, scatter(): lax.psum_scatter(array.astype(bf16), axis_name, scatter_dimension=axis, t...  171 us
    psum x1, waiting for transfers between devices, local(): lax.psum(scatter(one, 'narrow', axis).astype(bf16), 'wide').astype(f32)  126 us
    pallas_call x1, Pallas kernels, forward_call(): pl.pallas_call(forward_kernel, out_shape=(shape((2, FF, D), bf16), shape(...  58.9 us
    psum x1, blocking collectives, local(): lax.psum(scatter(one, 'narrow', axis).astype(bf16), 'wide').astype(f32)  43.8 us
    sub x2, matrix products, mix_back(): chance_slope - jnp.sum(chances * chance_slope, axis=-1, keepdims=True)  33.7 us
    dot_general x4, matrix products, dot_nt(): lax.dot_general(left, right, (((1,), (1,)), ((), ())), preferred_element_...  30.3 us
    unnamed x60, local copies, waits for them, and re-layouts  28.4 us
    dot_general x4, matrix products, dot_tn(): lax.dot_general(left, right, (((0,), (0,)), ((), ())), preferred_element_...  25.2 us
  transfers between devices with their start and end apart: 8, of which 6 were waited for; matrix products, arithmetic and copies ran while one was open for 26% of the time, Pallas kernels for 0%

profile of v1, /device:TPU:0, one launch (start us, length us, event | category | flops | bytes accessed | tf_op | source)
XLA Modules:
  0.0 640.1 jit_solution(13270087652461866605)
XLA Ops:
  13.8 58.9 %shard_map.237 = (bf16[2,3072,768]{2,1,0:T(8,128)(2,1)}, bf16[12,512,512]{2,1,0:T(8,128)(2,1)}, bf16[768,768]{1,0:T(8,128)(2,1)}, bf16[768,768]{1,0:T(8,128)(2,1...) custom-call(bf16[1024,768]{1,0:T(8,128)(2,1)} %bitcast.100, ...), custom_call_target="tpu_custom_call" | custom-call | tf_op jit(solution)/shard_map/pallas_call | solution.py:385
  77.9 7.4 %fusion.33 = f32[1024,3072]{1,0:T(8,128)S(1)} fusion(bf16[2,3072,768]{2,1,0:T(8,128)(2,1)} %get-tuple-element.62, f32[1024,768]{1,0:T(8,128)S(1)} %copy-done, f32[768]{0:T(1024)S(1)} %get-tuple-element.126, f32[768]{0:T(1024)S(1)} %get-tuple-element.127, f32[1024]{0:T(1024)S(1)} %add_rsqrt_fusion, f32[1024]{0:T(1024)S(1)} %broadcast_multiply_fusion.5), kind=kOutput, calls=%fused_computation.41 | convolution fusion | flops 4835770368 | bytes 20461568 | tf_op jit(solution)/shard_map/dot_general | solution.py:93
  85.2 4.6 copy-done.20
  89.8 9.4 %convolution_convert_fusion = bf16[3072,768]{1,0:T(8,128)(2,1)} fusion(bf16[1024,768]{1,0:T(8,128)(2,1)S(1)} %bitcast.107, f32[1024,3072]{1,0:T(8,128)S(1)} %fusion.33, f32[3072]{0:T(1024)S(1)} %add.117), kind=kOutput, calls=%fused_computation.33 | convolution fusion | flops 4865654784 | bytes 18886656 | tf_op jit(solution)/shard_map/dot_general | solution.py:97
  99.4 16.8 %fusion.48 = (bf16[3072]{0:T(1024)(128)(2,1)}, bf16[1024,3072]{1,0:T(8,128)(2,1)S(1)}) fusion(f32[1024,3072]{1,0:T(8,128)} %copy-done.20, f32[3072]{0:T(1024)S(1)} %add.117, bf16[1024,768]{1,0:T(8,128)(2,1)} %bitcast.106, bf16[2,3072,768]{2,1,0:T(8,128)(2,1)} %get-tuple-element.62), kind=kOutput, calls=%fused_computation.83 | convolution fusion | flops 4901041152 | bytes 25184256 | tf_op jit(solution)/shard_map/dot_general | solution.py:93
  116.2 2.7 copy-done.21
  118.9 7.6 %convolution_convert_fusion.1 = bf16[768,3072]{0,1:T(8,128)(2,1)} fusion(bf16[1024,3072]{1,0:T(8,128)(2,1)S(1)} %get-tuple-element.164, f32[1024,768]{1,0:T(8,128)S(1)} %copy-done, f32[768]{0:T(1024)S(1)} %get-tuple-element.126, f32[768]{0:T(1024)S(1)} %get-tuple-element.127, f32[1024]{0:T(1024)S(1)} %add_rsqrt_fusion, f32[1024]{0:T(1024)S(1)} %broadcast_multiply_fusion.5), kind=kOutput, calls=%fused_computation.34 | convolution fusion | flops 4838129664 | bytes 14170112 | tf_op jit(solution)/shard_map/dot_general | solution.py:97
  126.9 10.8 %multiply_reduce_fusion.1 = (bf16[768]{0:T(1024)(128)(2,1)}, f32[1024]{0:T(1024)S(1)}, f32[1024]{0:T(1024)S(1)}, bf16[768]{0:T(1024)(128)(2,1)}, f32[1024,768]{1,0:T(8,128)}) fusion(f32[1024,768]{1,0:T(8,128)S(1)} %copy-done, f32[1024]{0:T(1024)S(1)} %add_rsqrt_fusion, f32[1024]{0:T(1024)S(1)} %broadcast_multiply_fusion.5, f32[768]{0:T(1024)S(1)} %get-tuple-element.127, ...), kind=kOutput, calls=%fused_computation.51 | convolution fusion | flops 4838912000 | bytes 17324032 | tf_op jit(solution)/shard_map/dot_general | solution.py:89
  137.7 8.7 %copy.41 = bf16[12,512,512]{1,2,0:T(8,128)(2,1)} copy(bf16[12,512,512]{2,1,0:T(8,128)(2,1)} %get-tuple-element.113) | data formatting | bytes 12582912
  146.3 3.1 multiply_add_fusion
  149.5 2.6 convolution_convert_fusion.2
  152.1 61.5 %while.13 = (s32[]{:T(128)}, f32[12,512,512]{1,2,0:T(8,128)}, bf16[2,512,768]{2,1,0:T(8,128)(2,1)}, s32[2,512]{1,0:T(2,128)S(1)}, bf16[12,512,512]{1,2,0:T(8,128...) while((s32[]{:T(128)}, f32[12,512,512]{1,2,0:T(8,128)}, ...), condition=%wide.region_7.0_spmd.clone, body=%wide.region_4.7_spmd.clone.sunk | while | flops 1265238528 | bytes 57751672 | solution.py:494
  152.3 4.2 fusion.82
  158.0 5.2 fusion.83
  165.9 14.6 %select_add_fusion.2 = f32[12,512,512]{1,2,0:T(8,128)} fusion(f32[12,512,512]{1,2,0:T(8,128)} %get-tuple-element.224, pred[]{:T(512)S(6)} %compare.3, f32[12,512]{1,0:T(8,128)S(1)} %fusion.82, bf16[12,512,512]{1,2,0:T(8,128)(2,1)} %get-tuple-element.236, pred[512,512]{0,1:T(8,128)(4,1)S(1)} %broadcast_compare_fusion.2, ...), kind=kOutput, calls=%fused_computation.1.clone.1 | convolution fusion | flops 839916032 | bytes 33316864 | tf_op jit(solution)/shard_map/while/body/eval_jaxpr/sub | solution.py:483
  180.8 4.2 fusion.82
  186.4 5.1 fusion.83
  194.3 19.1 %select_add_fusion.2 = f32[12,512,512]{1,2,0:T(8,128)} fusion(f32[12,512,512]{1,2,0:T(8,128)} %get-tuple-element.224, pred[]{:T(512)S(6)} %compare.3, f32[12,512]{1,0:T(8,128)S(1)} %fusion.82, bf16[12,512,512]{1,2,0:T(8,128)(2,1)} %get-tuple-element.236, pred[512,512]{0,1:T(8,128)(4,1)S(1)} %broadcast_compare_fusion.2, ...), kind=kOutput, calls=%fused_computation.1.clone.1 | convolution fusion | flops 839916032 | bytes 33316864 | tf_op jit(solution)/shard_map/while/body/eval_jaxpr/sub | solution.py:483
  213.6 4.4 convolution_convert_fusion.4
  220.5 3.9 convolution_convert_fusion.3
  224.5 10.0 %copy.45 = bf16[12,512,512]{2,1,0:T(8,128)(2,1)} copy(f32[12,512,512]{1,2,0:T(8,128)} %get-tuple-element.68) | data formatting | bytes 18874368 | tf_op jit(solution)/shard_map/while | solution.py:494
  238.0 140.7 %reduce-scatter.18.cloned.1.call-done = bf16[768,192]{0,1:T(8,128)(2,1)} async-done(((bf16[768,3072]{0,1:T(8,128)(2,1)}), bf16[768,192]{0,1:T(8,128)(2,1)}) %reduce-scatter.18.cloned.1.call-update) | async-done | bytes 294928 | tf_op jit(solution)/shard_map/reduce_scatter | solution.py:506
  382.9 6.3 reduce-scatter.22.cloned.1.call-done
  391.3 10.6 %reduce-scatter.16.cloned.1.call-done = bf16[384,768]{1,0:T(8,128)(2,1)} async-done(((bf16[768,768]{1,0:T(8,128)(2,1)}), bf16[384,768]{1,0:T(8,128)(2,1)}) %reduce-scatter.16.cloned.1.call-update) | async-done | bytes 589840 | tf_op jit(solution)/shard_map/reduce_scatter | solution.py:506
  401.9 18.4 %reduce-scatter.14.cloned.1.call-done = bf16[12,256,512]{2,1,0:T(8,128)(2,1)} async-done(((bf16[12,512,512]{2,1,0:T(8,128)(2,1)}), bf16[12,256,512]{2,1,0:T(8,128)(2,1)}) %reduce-scatter.14.cloned.1.call-update) | async-done | bytes 3145744 | tf_op jit(solution)/shard_map/reduce_scatter | solution.py:506
  422.1 3.5 multiply_reduce_fusion.2
  425.6 3.3 all-reduce.8
  429.4 43.8 %all-reduce.6 = (bf16[384]{0:T(512)(128)(2,1)S(1)}, bf16[384]{0:T(512)(128)(2,1)S(1)}, bf16[384]{0:T(512)(128)(2,1)S(1)}, bf16[384]{0:T(512)(128)(2,1)S(1)}, bf1...) all-reduce(bf16[384]{0:T(512)(128)(2,1)S(1)} %dynamic-slice.1, ...), channel_id=1, replica_groups=mesh['narrow'=2,'wide'=16] {'wide'}, use_global_device_ids=true, to_apply=%region_20.21 | all-reduce | flops 3456 | bytes 13824 | tf_op jit(solution)/shard_map/psum | solution.py:518
  476.8 4.9 add_convert_fusion
  481.7 13.1 %add_convert_fusion.1 = bf16[1024,768]{1,0:T(8,128)(2,1)} fusion(f32[1024,768]{1,0:T(8,128)S(1)} %copy-done.1, bf16[2,3072,768]{2,1,0:T(8,128)(2,1)} %get-tuple-element.62, f32[768]{0:T(1024)S(1)} %copy-done.13, f32[1024,3072]{1,0:T(8,128)} %copy-done.20, f32[3072]{0:T(1024)S(1)} %copy-done.11), kind=kOutput, calls=%fused_computation.58 | convolution fusion | flops 4865654784 | bytes 22035456 | tf_op jit(solution)/shard_map/dot_general | solution.py:89
  498.4 126.3 %all-reduce.11.cloned.1.call-done = (bf16[12,256,512]{2,1,0:T(8,128)(2,1)}, bf16[768,384]{1,0:T(8,128)(2,1)}, bf16[384,768]{1,0:T(8,128)(2,1)}) async-done(((bf16[12,256,512]{2,1,0:T(8,128)(2,1)}, bf16[768,384]{1,0:T(8,128)(2,1)}, bf16[384,768]{1,0:T(8,128)(2,1)}), (bf16[12,256,512]{2,1,0:T(8,128)(2,1)}, bf16[768,384]{1,0:T(8,128)(2,1)}, bf16[384,768]{1,0:T(8,128)(2,1)})) %all-reduce.11.cloned.1.call-update) | async-done | bytes 4325392 | tf_op jit(solution)/shard_map/psum | solution.py:518
  629.2 3.6 convert_element_type.157
  (127 shorter events, 45.8 us)
Async XLA Ops:
  7.2 228.9 %reduce-scatter.20.cloned.1.call-start = ((), (), s32[]{:S(2)}) async-start(), calls=%async_computation.10 | async-start | bytes 5013504 | tf_op jit(solution)/shard_map/reduce_scatter | solution.py:506
  72.7 4.6 copy-start
  77.8 21.6 %copy-start.10 = (f32[3072]{0:T(1024)}, f32[3072]{0:T(1024)S(1)}, u32[]{:S(2)}) copy-start(f32[3072]{0:T(1024)S(1)} %add.117) | copy-start | bytes 36868
  77.9 12.0 %copy-start.5 = (bf16[2,512,768]{2,1,0:T(8,128)(2,1)S(1)}, bf16[2,512,768]{2,1,0:T(8,128)(2,1)}, u32[]{:S(2)}) copy-start(bf16[2,512,768]{2,1,0:T(8,128)(2,1)} %param.29) | copy-start | bytes 4718596
  85.2 4.6 copy-start.20
  99.2 279.5 %reduce-scatter.18.cloned.1.call-start = ((), (), s32[]{:S(2)}) async-start(), calls=%async_computation.9 | async-start | bytes 5013504 | tf_op jit(solution)/shard_map/reduce_scatter | solution.py:506
  116.2 2.7 copy-start.21
  126.6 262.6 %reduce-scatter.22.cloned.1.call-start = ((), (), s32[]{:S(2)}) async-start(), calls=%async_computation.11 | async-start | bytes 1769472
  146.3 3.2 copy-start.18
  149.5 2.6 copy-start.3
  149.5 2.6 copy-start.8
  217.9 2.6 copy-start.4
  220.5 181.4 %reduce-scatter.16.cloned.1.call-start = ((), (), s32[]{:S(2)}) async-start(), calls=%async_computation.8 | async-start | bytes 1769472 | tf_op jit(solution)/shard_map/reduce_scatter | solution.py:506
  224.5 195.9 %reduce-scatter.14.cloned.1.call-start = ((), (), s32[]{:S(2)}) async-start(), calls=%async_computation.7 | async-start | bytes 9437184 | tf_op jit(solution)/shard_map/reduce_scatter | solution.py:506
  234.5 146.2 %copy-start.6 = (bf16[2,512,768]{2,1,0:T(8,128)(2,1)S(1)}, bf16[2,512,768]{2,1,0:T(8,128)(2,1)}, u32[]{:S(2)}) copy-start(bf16[2,512,768]{2,1,0:T(8,128)(2,1)} %param.29) | copy-start | bytes 4718596
  234.5 146.5 %copy-start.19 = (u32[32]{0:T(128)S(1)}, u32[32]{0:T(128)}, u32[]{:S(2)}) copy-start(u32[32]{0:T(128)} %constant.53) | copy-start | bytes 388
  234.6 260.2 %reduce-scatter.26.cloned.1.call-start = ((), (), s32[]{:S(2)}) async-start(), calls=%async_computation.13 | async-start | bytes 589824
  238.0 258.6 %reduce-scatter.24.cloned.1.call-start = ((), (), s32[]{:S(2)}) async-start(), calls=%async_computation.12 | async-start | bytes 589824
  380.6 244.1 %all-reduce.11.cloned.1.call-start = ((), (), s32[]{:S(2)}) async-start(), calls=%async_computation.14 | async-start | bytes 8650752 | tf_op jit(solution)/shard_map/psum | solution.py:518
  381.0 39.3 %copy-start.2 = (bf16[2,512,768]{2,1,0:T(8,128)(2,1)S(1)}, bf16[2,512,768]{2,1,0:T(8,128)(2,1)}, u32[]{:S(2)}) copy-start(bf16[2,512,768]{2,1,0:T(8,128)(2,1)} %param.16) | copy-start | bytes 4718596
  420.3 1.0 copy-start.9
  420.3 1.4 copy-start.16
  420.3 1.7 copy-start.17
  422.1 3.5 copy-start.12
  422.1 3.5 copy-start.14
  422.1 3.5 copy-start.15
  476.7 4.9 copy-start.1
  476.7 4.9 copy-start.11
  476.7 4.9 copy-start.13
  624.7 4.5 copy-start.7
Sparse Core Ops, SparseCore 0:
  99.3 136.7 reduce-scatter.19
  242.1 136.6 reduce-scatter.17
  381.6 7.6 reduce-scatter.21
  392.0 9.8 reduce-scatter.15
  404.6 15.6 reduce-scatter.13
  422.5 8.9 reduce-scatter.25
  433.7 8.9 reduce-scatter.23
  450.4 174.2 all-reduce.10

commit v2 on v1

--- a/solution.py
+++ b/solution.py
@@ -407,6 +407,318 @@
     )(x, documents, mixing, value_weight, output_weight, shard, vectors)
 
 
+def gelu_and_slope(v):
+    scale = 0.7978845608028654
+    square = v * v
+    t = jnp.tanh(scale * v * (1.0 + 0.044715 * square))
+    rise = 0.5 * (1.0 + t)
+    slope = rise + 0.5 * scale * v * (1.0 - t * t) * (1.0 + 3.0 * 0.044715 * square)
+    return v * rise, slope
+
+
+def norm_slope(slope, unit, reciprocal, gain):
+    tilted = slope * gain
+    centered = tilted - jnp.mean(tilted, axis=-1, keepdims=True)
+    centered = centered - unit * jnp.mean(tilted * unit, axis=-1, keepdims=True)
+    return centered * reciprocal
+
+
+def dense_kernel(
+    middle_ref, cotangent_ref, blended_ref, output_ref, vector_ref, full_ref,
+    result_out, slope_out, blended_slope_out, output_grad_out, sums_out, hidden_out, down_out,
+    normed, total, slope, active, hidden_slope, weight, grads, to_twin, from_twin, part,
+    first_y, first_x, second_x, second_y, line_in, sums,
+    weight_sem, twin_sent, twin_recv, first_y_sent, first_y_recv, first_x_sent, first_x_recv,
+    second_x_sent, second_x_recv, second_y_sent, second_y_recv, up_sent, down_sent, line_recv, out_sem,
+):
+    core, x, y, z = place()
+    mine, other = halves(core)
+    near_x, near_y = seat(core, 1 - x, y, z), seat(core, x, 1 - y, z)
+    above, below = seat(core, x, y, z + 1), seat(core, x, y, z - 1)
+    twin = seat(1 - core, x, y, z)
+    tokens = middle_ref.shape[0]
+    block = 256
+    order = (0, 3, 1, 2)
+
+    def load(i):
+        rows = pl.ds(order[i] * GROUP, GROUP)
+        return pltpu.make_async_copy(full_ref.at[:, rows], weight.at[i % 2], weight_sem.at[i % 2])
+
+    load(0).start()
+    greet(core, x, y, z)
+
+    def twin_copy(i, m):
+        k = order[i]
+        return remote(
+            to_twin.at[i % 2, m], from_twin.at[k, m], twin_sent.at[k, m], twin_recv.at[k, m], twin
+        )
+
+    def first_copy(k, m):
+        if m == 0:
+            return remote(
+                part.at[k, 0, 1 - y], first_y.at[k], first_y_sent.at[k], first_y_recv.at[k], near_y
+            )
+        return remote(
+            part.at[k, 1, :, 1 - x], first_x.at[k], first_x_sent.at[k], first_x_recv.at[k], near_x
+        )
+
+    def second_copy(k, m):
+        if m == 0:
+            return remote(
+                part.at[k, 0, y, 1 - x], second_x.at[k], second_x_sent.at[k], second_x_recv.at[k], near_x
+            )
+        return remote(
+            part.at[k, 1, 1 - y, x], second_y.at[k], second_y_sent.at[k], second_y_recv.at[k], near_y
+        )
+
+    def line_copy(k, m, up):
+        src = part.at[k, m, y, x]
+        if up:
+            return remote(src, line_in.at[0, k, m], up_sent.at[k, m], line_recv.at[0, k, m], above)
+        return remote(src, line_in.at[1, k, m], down_sent.at[k, m], line_recv.at[1, k, m], below)
+
+    def add_in(k, m, y_of, x_of, got):
+        part[k, m, y_of, x_of] = (part[k, m, y_of, x_of].astype(f32) + got.astype(f32)).astype(bf16)
+
+    def twin_event(i):
+        for m in range(2):
+            if i >= 2:
+                twin_copy(i - 2, m).wait_send()
+            to_twin[i % 2, m] = grads[m, :, other].astype(bf16)
+            twin_copy(i, m).start()
+
+    def sum_event(i):
+        k = order[i]
+        for m in range(2):
+            twin_copy(i, m).wait_recv()
+            both = grads[m, :, mine] + from_twin[k, m].astype(f32)
+            part[k, m] = both.astype(bf16).reshape(2, 2, CHUNK, HALF)
+            first_copy(k, m).start()
+
+    def second_event(i):
+        k = order[i]
+        first_copy(k, 0).wait_recv()
+        add_in(k, 0, y, 1 - x, first_y[k, 1 - x])
+        second_copy(k, 0).start()
+        first_copy(k, 1).wait_recv()
+        add_in(k, 1, 1 - y, x, first_x[k, 1 - y])
+        second_copy(k, 1).start()
+        add_in(k, 0, y, x, first_y[k, x])
+        add_in(k, 1, y, x, first_x[k, y])
+
+    def line_event(i):
+        k = order[i]
+        second_copy(k, 0).wait_recv()
+        add_in(k, 0, y, x, second_x[k])
+        second_copy(k, 1).wait_recv()
+        add_in(k, 1, y, x, second_y[k])
+        hop_event(i, 0)
+
+    def hop_event(i, hop):
+        k = order[i]
+        if hop < k:
+
+            @pl.when(z == hop)
+            def _():
+                for m in range(2):
+                    if hop > 0:
+                        line_copy(k, m, True).wait_recv()
+                        add_in(k, m, y, x, line_in[0, k, m])
+                    line_copy(k, m, True).start()
+
+        if hop < 3 - k:
+
+            @pl.when(z == 3 - hop)
+            def _():
+                for m in range(2):
+                    if hop > 0:
+                        line_copy(k, m, False).wait_recv()
+                        add_in(k, m, y, x, line_in[1, k, m])
+                    line_copy(k, m, False).start()
+
+        if hop == max(k, 3 - k):
+
+            @pl.when(z == k)
+            def _():
+                for m, out in enumerate((hidden_out, down_out)):
+                    both = part[k, m, y, x].astype(f32)
+                    if k > 0:
+                        line_copy(k, m, True).wait_recv()
+                        both = both + line_in[0, k, m].astype(f32)
+                    if k < 3:
+                        line_copy(k, m, False).wait_recv()
+                        both = both + line_in[1, k, m].astype(f32)
+                    out[...] = both
+
+    gain, shift, down_bias = vector_ref[2:3, :], vector_ref[3:4, :], vector_ref[4:5, :]
+
+    def rows_of(b):
+        return pl.ds(pl.multiple_of(b * block, block), block)
+
+    def second_norm(b, _):
+        rows = rows_of(b)
+        unit, _r = unit_of(middle_ref[rows, :])
+        normed[rows, :] = (unit * gain + shift).astype(bf16)
+        return 0
+
+    lax.fori_loop(0, tokens // block, second_norm, 0)
+    sums[...] = jnp.zeros_like(sums)
+
+    def dense_block(i, bias, b, _):
+        k = order[i]
+        rows = rows_of(b)
+        low, cot = normed[rows, :], cotangent_ref[rows, :]
+        hidden = dot_nt(low, weight[i % 2, 0]) + bias
+        pulled = dot_nt(cot, weight[i % 2, 1])
+        act, pull = gelu_and_slope(hidden)
+        act = act.astype(bf16)
+        turned = (pulled * pull).astype(bf16)
+        active[rows, :] = act
+        hidden_slope[rows, :] = turned
+        sums[3 + k : 4 + k, :] += jnp.sum(turned.astype(f32), axis=0, keepdims=True)
+        down = dot_nn(act, weight[i % 2, 1])
+        back = dot_nn(turned, weight[i % 2, 0])
+        if i == 0:
+            total[rows, :] = middle_ref[rows, :] + down_bias + down
+            slope[rows, :] = back
+            sums[0:1, :] += jnp.sum(cot.astype(f32), axis=0, keepdims=True)
+        else:
+            total[rows, :] += down
+            slope[rows, :] += back
+        return 0
+
+    def grad_rows(m, b, _):
+        lanes = rows_of(b)
+        left, right = (hidden_slope, normed) if m == 0 else (active, cotangent_ref)
+        grads[m, lanes, :] = dot_tn(left[:, lanes], right[...])
+        return 0
+
+    for i in range(4):
+        bias_rows = 5 + 2 * (order[i] % 2)
+        lanes = slice((order[i] // 2) * HALF, (order[i] // 2 + 1) * HALF)
+        bias = jnp.concatenate(
+            [vector_ref[bias_rows : bias_rows + 1, lanes], vector_ref[bias_rows + 1 : bias_rows + 2, lanes]],
+            axis=1,
+        )
+        load(i).wait()
+        if i < 3:
+            load(i + 1).start()
+        lax.fori_loop(0, 2, functools.partial(dense_block, i, bias), 0)
+        if i >= 1:
+            sum_event(i - 1)
+        if i >= 2:
+            line_event(i - 2)
+        if i >= 3:
+            hop_event(i - 3, 2)
+        lax.fori_loop(2, 4, functools.partial(dense_block, i, bias), 0)
+        for m in range(2):
+            lax.fori_loop(0, GROUP // block, functools.partial(grad_rows, m), 0)
+        twin_event(i)
+        if i >= 1:
+            second_event(i - 1)
+        if i >= 2:
+            hop_event(i - 2, 1)
+        if i >= 3:
+            hop_event(i - 3, 3)
+
+    def finish(b, _):
+        rows = rows_of(b)
+        unit, reciprocal = unit_of(middle_ref[rows, :])
+        raw = slope[rows, :]
+        sums[1:2, :] += jnp.sum(raw * unit, axis=0, keepdims=True)
+        sums[2:3, :] += jnp.sum(raw, axis=0, keepdims=True)
+        moved = cotangent_ref[rows, :].astype(f32) + norm_slope(raw, unit, reciprocal, gain)
+        slope[rows, :] = moved
+        low = moved.astype(bf16)
+        active[rows, :] = low
+        hidden_slope[rows, :] = dot_nt(low, output_ref[...]).astype(bf16)
+        result_out[rows, :] = total[rows, :].astype(bf16)
+        return 0
+
+    lax.fori_loop(0, 2, finish, 0)
+    sum_event(3)
+    line_event(2)
+    hop_event(1, 2)
+    lax.fori_loop(2, 4, finish, 0)
+    outs = [
+        pltpu.make_async_copy(slope, slope_out, out_sem.at[0]),
+        pltpu.make_async_copy(hidden_slope, blended_slope_out, out_sem.at[1]),
+        pltpu.make_async_copy(grads.at[0], output_grad_out, out_sem.at[2]),
+    ]
+    outs[0].start()
+    outs[1].start()
+
+    def project_grad(b, _):
+        lanes = rows_of(b)
+        grads[0, lanes, :] = dot_tn(blended_ref[:, lanes], active[...])
+        return 0
+
+    lax.fori_loop(0, D // block, project_grad, 0)
+    outs[2].start()
+    sums_out[...] = sums[...]
+    second_event(3)
+    hop_event(2, 1)
+    hop_event(1, 3)
+    line_event(3)
+    hop_event(2, 2)
+    hop_event(3, 1)
+    hop_event(3, 2)
+    for copy in outs:
+        copy.wait()
+    for i in range(4):
+        k = order[i]
+        for m in range(2):
+            if i >= 2:
+                twin_copy(i, m).wait_send()
+            first_copy(k, m).wait_send()
+            second_copy(k, m).wait_send()
+            if k > 0:
+
+                @pl.when(z < k)
+                def _():
+                    line_copy(k, m, True).wait_send()
+
+            if k < 3:
+
+                @pl.when(z > k)
+                def _():
+                    line_copy(k, m, False).wait_send()
+
+
+def dense_call(middle, cotangent, blended, output_full, vectors, full):
+    tokens = middle.shape[0]
+    any_spec = pl.BlockSpec(memory_space=pl.ANY)
+    vmem = pl.BlockSpec(memory_space=pltpu.VMEM)
+    shape = jax.ShapeDtypeStruct
+    dma = pltpu.SemaphoreType.DMA
+    piece = (CHUNK, HALF)
+    return pl.pallas_call(
+        dense_kernel,
+        out_shape=(
+            shape((tokens, D), bf16), shape((tokens, D), f32), shape((tokens, D), bf16),
+            shape((D, D), f32), shape((8, D), f32), shape(piece, f32), shape(piece, f32),
+        ),
+        in_specs=[vmem] * 5 + [any_spec],
+        out_specs=[vmem, any_spec, any_spec, any_spec, vmem, vmem, vmem],
+        scratch_shapes=[
+            pltpu.VMEM((tokens, D), bf16), pltpu.VMEM((tokens, D), f32), pltpu.VMEM((tokens, D), f32),
+            pltpu.VMEM((tokens, GROUP), bf16), pltpu.VMEM((tokens, GROUP), bf16),
+            pltpu.VMEM((2, 2, GROUP, D), bf16), pltpu.VMEM((2, GROUP, D), f32),
+            pltpu.VMEM((2, 2, GROUP, HALF), bf16), pltpu.VMEM((4, 2, GROUP, HALF), bf16),
+            pltpu.VMEM((4, 2, 2, 2) + piece, bf16),
+            pltpu.VMEM((4, 2) + piece, bf16), pltpu.VMEM((4, 2) + piece, bf16),
+            pltpu.VMEM((4,) + piece, bf16), pltpu.VMEM((4,) + piece, bf16),
+            pltpu.VMEM((2, 4, 2) + piece, bf16), pltpu.VMEM((8, D), f32),
+            dma((2,)), dma((4, 2)), dma((4, 2)), dma((4,)), dma((4,)), dma((4,)), dma((4,)),
+            dma((4,)), dma((4,)), dma((4,)), dma((4,)), dma((4, 2)), dma((4, 2)), dma((2, 4, 2)),
+            dma((3,)),
+        ],
+        compiler_params=pltpu.CompilerParams(
+            collective_id=1, has_side_effects=True, vmem_limit_bytes=60 << 20
+        ),
+    )(middle, cotangent, blended, output_full, vectors, full)
+
+
 def contract_rows(left_side, right_side):
     return dot_tn(left_side, right_side)
 
@@ -440,33 +752,15 @@
     ) = forward_call(
         inputs.reshape(tokens, D), documents, mixing, value_weight, output_weight, shard, vectors
     )
-    gain_first, shift_first, gain_second, shift_second, bias_down = (vector_full[n] for n in range(5))
-    bias_hidden = vector_full[5:9].reshape(4, 2, HALF).swapaxes(0, 1).reshape(FF)
-    hidden_t, down_full = full[0], full[1]
+    gain_first = vector_full[0]
     stream = inputs.reshape(tokens, D).astype(f32)
     unit_first, recip_first = unit_of(stream)
-    unit_second, recip_second = unit_of(middle)
-    normed_two_low = (unit_second * gain_second + shift_second).astype(bf16)
-    hidden = dot_nt(normed_two_low, hidden_t) + bias_hidden
-    activated, gelu_pull = jax.vjp(jax.nn.gelu, hidden)
-    active = activated.astype(jnp.bfloat16)
-    result = middle + dot_nn(active, down_full) + bias_down
-    slope_low = cotangent.reshape(tokens, D)
-    slope_wide = slope_low.astype(jnp.float32)
-    down_bias_sum = jnp.sum(slope_wide, axis=0)
-    down_grad = contract_rows(active, slope_low)
-    active_slope = dot_nt(slope_low, down_full)
-    hidden_slope = gelu_pull(active_slope)[0].astype(bf16)
-    hidden_bias_sum = jnp.sum(hidden_slope.astype(jnp.float32), axis=0)
-    hidden_grad = contract_rows(normed_two_low, hidden_slope)
-    normed_two_slope = dot_nn(hidden_slope, hidden_t)
-    back_second, gain_second_sum, shift_second_sum = norm_back(
-        normed_two_slope, unit_second, recip_second, gain_second
-    )
-    middle_slope = slope_wide + back_second
-    attended_slope = middle_slope.astype(jnp.bfloat16)
-    output_grad = contract_rows(blended, attended_slope)
-    blended_slope = dot_nt(attended_slope, output_full).astype(jnp.bfloat16)
+    (
+        result, middle_slope, blended_slope, output_grad, sums_two, hidden_share, down_share,
+    ) = dense_call(middle, cotangent.reshape(tokens, D), blended, output_full, vector_full, full)
+    hidden_share = hidden_share.T
+    down_bias_sum, gain_second_sum, shift_second_sum = (sums_two[n] for n in range(3))
+    hidden_bias_sum = sums_two[3:7].reshape(FF)
     value_rows = values.reshape(row_count, SEQ, D)
 
     def mix_back(running, bundle):
@@ -507,8 +801,6 @@
             array.astype(bf16), axis_name, scatter_dimension=axis, tiled=True
         ).astype(f32)
 
-    hidden_share = scatter(scatter(hidden_grad, "wide", 1), "narrow", 0)
-    down_share = scatter(scatter(down_grad, "wide", 0), "narrow", 1)
     sums = (
         (mixing_grad, 1), (value_grad, 1), (output_grad, 0), (gain_first_sum, 0),
         (shift_first_sum, 0), (gain_second_sum, 0), (shift_second_sum, 0), (hidden_bias_sum, 0),
@@ -519,7 +811,7 @@
         for one, axis in sums
     ]
     return (
-        result.reshape(row_count, SEQ, D).astype(jnp.bfloat16),
+        result.reshape(row_count, SEQ, D),
         inputs_slope.reshape(row_count, SEQ, D),
         *totals[:7], hidden_share, totals[7], down_share, totals[8],
     )

time: 649 us -> 473 us (0.73)
  waiting for transfers between devices: 304 us -> 148 us
  Pallas kernels: 58.9 us -> 132 us
  matrix products: 123 us -> 52.4 us
  local copies, waits for them, and re-layouts: 53.4 us -> 39.8 us
  other arithmetic: 36 us -> 28.6 us
    reduce_scatter x4 -> x2, waiting for transfers between devices: 171 us -> 29.3 us  [scatter(): lax.psum_scatter(array.astype(bf16), axis_name, scatter_dimension=axis, t...]
    pallas_call x0 -> x1, Pallas kernels: none -> 73.5 us  [dense_call(): pl.pallas_call(dense_kernel, out_shape=(shape((tokens, D), bf16), shape((...]
    dot_general x4 -> x1, matrix products: 30.3 us -> 4.72 us  [dot_nt(): lax.dot_general(left, right, (((1,), (1,)), ((), ())), preferred_element_...]
    dot_general x2 -> x0, matrix products: 23.9 us -> none  [dot_nn(): lax.dot_general(left, right, (((1,), (0,)), ((), ())), preferred_element_...]
    dot_general x4 -> x1, matrix products: 25.2 us -> 3.32 us  [dot_tn(): lax.dot_general(left, right, (((0,), (0,)), ((), ())), preferred_element_...]
    unnamed x60 -> x37, local copies, waits for them, and re-layouts: 28.4 us -> 16.4 us
    psum x1, waiting for transfers between devices: 126 us -> 117 us  [local(): lax.psum(scatter(one, 'narrow', axis).astype(bf16), 'wide').astype(f32)]
  transfers between devices with their start and end apart: 8 -> 4, of which waited for: 6 -> 4; matrix products, arithmetic and copies ran while one was open for 26% -> 6% of each run, Pallas kernels for 0% -> 0%
where the time goes in v2:
time: 473 us; the launch traced here: 467 us
  waiting for transfers between devices  148 us (31%)
  Pallas kernels  132 us (28%)
  matrix products  52.4 us (11%)
  blocking collectives  49.6 us (10%)
  local copies, waits for them, and re-layouts  39.8 us (8%)
  other arithmetic  28.6 us (6%)
  between operations  15.5 us (3%)
    psum x1, waiting for transfers between devices, local(): lax.psum(scatter(one, 'narrow', axis).astype(bf16), 'wide').astype(f32)  117 us
    pallas_call x1, Pallas kernels, dense_call(): pl.pallas_call(dense_kernel, out_shape=(shape((tokens, D), bf16), shape((...  73.5 us
    pallas_call x1, Pallas kernels, forward_call(): pl.pallas_call(forward_kernel, out_shape=(shape((2, FF, D), bf16), shape(...  58.8 us
    psum x1, blocking collectives, local(): lax.psum(scatter(one, 'narrow', axis).astype(bf16), 'wide').astype(f32)  46.2 us
    sub x2, matrix products, mix_back(): chance_slope - jnp.sum(chances * chance_slope, axis=-1, keepdims=True)  34.1 us
    reduce_scatter x2, waiting for transfers between devices, scatter(): lax.psum_scatter(array.astype(bf16), axis_name, scatter_dimension=axis, t...  29.3 us
    unnamed x37, local copies, waits for them, and re-layouts  16.4 us
    convert_element_type x9, other arithmetic, local(): lax.psum(scatter(one, 'narrow', axis).astype(bf16), 'wide').astype(f32)  11.2 us
  transfers between devices with their start and end apart: 4, of which 4 were waited for; matrix products, arithmetic and copies ran while one was open for 6% of the time, Pallas kernels for 0%

profile of v2, /device:TPU:0, one launch (start us, length us, event | category | flops | bytes accessed | tf_op | source)
XLA Modules:
  0.0 467.2 jit_solution(11735029797068398834)
XLA Ops:
  12.1 1.7 pad_maximum_fusion.shard_ref
  13.9 58.8 %shard_map.237 = (bf16[2,3072,768]{2,1,0:T(8,128)(2,1)}, bf16[12,512,512]{2,1,0:T(8,128)(2,1)}, bf16[768,768]{1,0:T(8,128)(2,1)}, bf16[768,768]{1,0:T(8,128)(2,1...) custom-call(bf16[1024,768]{1,0:T(8,128)(2,1)} %bitcast.57, ...), custom_call_target="tpu_custom_call" | custom-call | tf_op jit(solution)/shard_map/pallas_call | solution.py:385
  72.7 8.6 %copy.39 = bf16[12,512,512]{1,2,0:T(8,128)(2,1)} copy(bf16[12,512,512]{2,1,0:T(8,128)(2,1)} %get-tuple-element.127) | data formatting | bytes 12582912
  81.3 73.5 %shard_map.238 = (bf16[1024,768]{1,0:T(8,128)(2,1)}, f32[1024,768]{1,0:T(8,128)}, bf16[1024,768]{1,0:T(8,128)(2,1)}, f32[768,768]{1,0:T(8,128)}, f32[8,768]{1,0:...) custom-call(f32[1024,768]{1,0:T(8,128)} %get-tuple-element.67.middle_ref, bf16[1024,768]{1,0:T(8,128)(2,1)} %bitcast.65, ...), custom_call_target="tpu_custom_call" | custom-call | tf_op jit(solution)/shard_map/pallas_call | solution.py:695
  154.9 61.4 %while.13 = (s32[]{:T(128)}, f32[12,512,512]{1,2,0:T(8,128)}, bf16[2,512,768]{2,1,0:T(8,128)(2,1)}, s32[2,512]{1,0:T(2,128)S(1)}, bf16[12,512,512]{1,2,0:T(8,128...) while((s32[]{:T(128)}, f32[12,512,512]{1,2,0:T(8,128)}, ...), condition=%wide.region_3.4_spmd.clone, body=%wide.region_0.3_spmd.clone.sunk | while | flops 1265238528 | bytes 57751672 | solution.py:788
  155.1 4.1 fusion.47
  159.2 1.2 constant_dynamic-slice_fusion.6
  160.7 5.1 %fusion.48 = bf16[12,64,512]{2,1,0:T(8,128)(2,1)S(1)} fusion(bf16[512,12,64]{0,2,1:T(8,128)(2,1)S(1)} %bitcast.58, f32[12,512]{1,0:T(8,128)S(1)} %fusion.47, bf16[12,512,512]{1,2,0:T(8,128)(2,1)} %get-tuple-element.242, pred[512,512]{0,1:T(8,128)(4,1)S(1)} %broadcast_compare_fusion.2), kind=kOutput, calls=%fused_computation.9.clone.1 | convolution fusion | flops 415629312 | bytes 8151040 | tf_op jit(solution)/shard_map/while/body/eval_jaxpr/hij,ihd->jhd/dot_general | solution.py:779
  166.1 2.1 constant_dynamic-update-slice_fusion.2
  168.5 14.8 %select_add_fusion.2 = f32[12,512,512]{1,2,0:T(8,128)} fusion(f32[12,512,512]{1,2,0:T(8,128)} %get-tuple-element.230, pred[]{:T(512)S(6)} %compare.3, f32[12,512]{1,0:T(8,128)S(1)} %fusion.47, bf16[12,512,512]{1,2,0:T(8,128)(2,1)} %get-tuple-element.242, pred[512,512]{0,1:T(8,128)(4,1)S(1)} %broadcast_compare_fusion.2, ...), kind=kOutput, calls=%fused_computation.1.clone.1 | convolution fusion | flops 839916032 | bytes 33316864 | tf_op jit(solution)/shard_map/while/body/eval_jaxpr/sub | solution.py:777
  183.5 4.1 fusion.47
  187.7 1.2 constant_dynamic-slice_fusion.6
  189.1 5.1 %fusion.48 = bf16[12,64,512]{2,1,0:T(8,128)(2,1)S(1)} fusion(bf16[512,12,64]{0,2,1:T(8,128)(2,1)S(1)} %bitcast.58, f32[12,512]{1,0:T(8,128)S(1)} %fusion.47, bf16[12,512,512]{1,2,0:T(8,128)(2,1)} %get-tuple-element.242, pred[512,512]{0,1:T(8,128)(4,1)S(1)} %broadcast_compare_fusion.2), kind=kOutput, calls=%fused_computation.9.clone.1 | convolution fusion | flops 415629312 | bytes 8151040 | tf_op jit(solution)/shard_map/while/body/eval_jaxpr/hij,ihd->jhd/dot_general | solution.py:779
  194.6 2.1 constant_dynamic-update-slice_fusion.2
  197.0 19.3 %select_add_fusion.2 = f32[12,512,512]{1,2,0:T(8,128)} fusion(f32[12,512,512]{1,2,0:T(8,128)} %get-tuple-element.230, pred[]{:T(512)S(6)} %compare.3, f32[12,512]{1,0:T(8,128)S(1)} %fusion.47, bf16[12,512,512]{1,2,0:T(8,128)(2,1)} %get-tuple-element.242, pred[512,512]{0,1:T(8,128)(4,1)S(1)} %broadcast_compare_fusion.2, ...), kind=kOutput, calls=%fused_computation.1.clone.1 | convolution fusion | flops 839916032 | bytes 33316864 | tf_op jit(solution)/shard_map/while/body/eval_jaxpr/sub | solution.py:777
  216.3 3.3 convolution_convert_fusion
  219.6 1.5 copy.45
  221.7 1.1 convert_element_type.119
  222.9 10.0 %copy.43 = bf16[12,512,512]{2,1,0:T(8,128)(2,1)} copy(f32[12,512,512]{1,2,0:T(8,128)} %get-tuple-element.79) | data formatting | bytes 18874368 | tf_op jit(solution)/shard_map/while | solution.py:788
  233.2 2.2 reduce-scatter.10.cloned.1.call-done
  235.4 2.1 copy.46
  237.6 10.7 %reduce-scatter.8.cloned.1.call-done = bf16[384,768]{1,0:T(8,128)(2,1)} async-done(((bf16[768,768]{1,0:T(8,128)(2,1)}), bf16[384,768]{1,0:T(8,128)(2,1)}) %reduce-scatter.8.cloned.1.call-update) | async-done | bytes 589840 | tf_op jit(solution)/shard_map/reduce_scatter | solution.py:800
  248.2 18.6 %reduce-scatter.6.cloned.1.call-done = bf16[12,256,512]{2,1,0:T(8,128)(2,1)} async-done(((bf16[12,512,512]{2,1,0:T(8,128)(2,1)}), bf16[12,256,512]{2,1,0:T(8,128)(2,1)}) %reduce-scatter.6.cloned.1.call-update) | async-done | bytes 3145744 | tf_op jit(solution)/shard_map/reduce_scatter | solution.py:800
  269.9 4.7 %multiply_reduce_fusion.1 = (bf16[768]{0:T(1024)(128)(2,1)S(1)}, f32[1024]{0:T(1024)S(1)}, f32[1024]{0:T(1024)S(1)}, bf16[768]{0:T(1024)(128)(2,1)S(1)}, f32[1024,768]{1,0:T(8,128)}) fusion(f32[1024]{0:T(1024)S(1)} %bitcast.73, f32[1024]{0:T(1024)S(1)} %bitcast.75, bf16[2,512,768]{2,1,0:T(8,128)(2,1)S(1)} %copy-done, f32[768]{0:T(1024)S(1)} %slice_reduce_fusion.3, ...), kind=kOutput, calls=%fused_computation.22 | convolution fusion | flops 1215820288 | bytes 7493632 | tf_op jit(solution)/shard_map/dot_general | solution.py:93
  274.6 3.3 all-reduce.8
  279.1 46.2 %all-reduce.6 = (bf16[384]{0:T(512)(128)(2,1)S(1)}, bf16[384]{0:T(512)(128)(2,1)S(1)}, bf16[384]{0:T(512)(128)(2,1)S(1)}, bf16[384]{0:T(512)(128)(2,1)S(1)}, bf1...) all-reduce(bf16[384]{0:T(512)(128)(2,1)S(1)} %dynamic-slice.1, ...), channel_id=1, replica_groups=mesh['narrow'=2,'wide'=16] {'wide'}, use_global_device_ids=true, to_apply=%region_16.17 | all-reduce | flops 3456 | bytes 13824 | tf_op jit(solution)/shard_map/psum | solution.py:810
  328.8 4.3 add_convert_fusion
  333.2 116.9 %all-reduce.11.cloned.1.call-done = (bf16[12,256,512]{2,1,0:T(8,128)(2,1)}, bf16[768,384]{1,0:T(8,128)(2,1)}, bf16[384,768]{1,0:T(8,128)(2,1)}) async-done(((bf16[12,256,512]{2,1,0:T(8,128)(2,1)}, bf16[768,384]{1,0:T(8,128)(2,1)}, bf16[384,768]{1,0:T(8,128)(2,1)}), (bf16[12,256,512]{2,1,0:T(8,128)(2,1)}, bf16[768,384]{1,0:T(8,128)(2,1)}, bf16[384,768]{1,0:T(8,128)(2,1)})) %all-reduce.11.cloned.1.call-update) | async-done | bytes 4325392 | tf_op jit(solution)/shard_map/psum | solution.py:810
  450.1 5.6 %convert_element_type.116 = f32[12,256,512]{2,1,0:T(8,128)} convert(bf16[12,256,512]{2,1,0:T(8,128)(2,1)} %get-tuple-element.157) | non-fusion elementwise | flops 1572864 | bytes 9437184 | tf_op jit(solution)/shard_map/convert_element_type | solution.py:810
  455.6 1.1 convert_element_type.118
  456.7 1.1 convert_element_type.120
  457.8 1.1 copy.75
  (78 shorter events, 15.8 us)
Async XLA Ops:
  7.2 228.3 %reduce-scatter.10.cloned.1.call-start = ((), (), s32[]{:S(2)}) async-start(), calls=%async_computation.5 | async-start | bytes 1769472
  81.3 73.5 %copy-start.7 = (s32[2,512]{1,0:T(2,128)S(1)}, s32[2,512]{1,0:T(2,128)}, u32[]{:S(2)}) copy-start(s32[2,512]{1,0:T(2,128)} %docs_ref.1) | copy-start | bytes 12292
  219.6 2.1 copy-start.1
  221.1 27.1 %reduce-scatter.8.cloned.1.call-start = ((), (), s32[]{:S(2)}) async-start(), calls=%async_computation.4 | async-start | bytes 1769472 | tf_op jit(solution)/shard_map/reduce_scatter | solution.py:800
  222.9 43.9 %reduce-scatter.6.cloned.1.call-start = ((), (), s32[]{:S(2)}) async-start(), calls=%async_computation.3 | async-start | bytes 9437184 | tf_op jit(solution)/shard_map/reduce_scatter | solution.py:800
  232.9 33.9 %copy-start = (bf16[2,512,768]{2,1,0:T(8,128)(2,1)S(1)}, bf16[2,512,768]{2,1,0:T(8,128)(2,1)}, u32[]{:S(2)}) copy-start(bf16[2,512,768]{2,1,0:T(8,128)(2,1)} %param.16) | copy-start | bytes 4718596
  232.9 217.1 %all-reduce.11.cloned.1.call-start = ((), (), s32[]{:S(2)}) async-start(), calls=%async_computation.6 | async-start | bytes 8650752 | tf_op jit(solution)/shard_map/psum | solution.py:810
  266.8 1.0 copy-start.8
  266.8 1.0 copy-start.10
  266.8 3.1 copy-start.9
  450.1 5.6 %copy-start.4 = (bf16[768,384]{1,0:T(8,128)(2,1)S(1)}, bf16[768,384]{1,0:T(8,128)(2,1)}, u32[]{:S(2)}) copy-start(bf16[768,384]{1,0:T(8,128)(2,1)} %get-tuple-element.158) | copy-start | bytes 1769476
  450.1 6.7 %copy-start.3 = (bf16[384,768]{1,0:T(8,128)(2,1)S(1)}, bf16[384,768]{1,0:T(8,128)(2,1)}, u32[]{:S(2)}) copy-start(bf16[384,768]{1,0:T(8,128)(2,1)} %get-tuple-element.159) | copy-start | bytes 1769476
  455.6 2.2 copy-start.2
  455.6 3.3 copy-start.6
  456.7 3.0 copy-start.5
Sparse Core Ops, SparseCore 0:
  221.2 14.1 reduce-scatter.9
  238.3 9.8 reduce-scatter.7
  251.1 15.6 reduce-scatter.5
  274.4 175.6 all-reduce.10

commit v3 on v2

--- a/solution.py
+++ b/solution.py
@@ -43,9 +43,10 @@
     )
 
 
-def greet(core, x, y, z):
+def greet(core, x, y, z, more=()):
     barrier = pltpu.get_barrier_semaphore()
-    for device in (seat(1 - core, x, y, z), seat(core, 1 - x, y, z), seat(core, x, 1 - y, z)):
+    near = (seat(1 - core, x, y, z), seat(core, 1 - x, y, z), seat(core, x, 1 - y, z)) + more
+    for device in near:
         pl.semaphore_signal(barrier, inc=1, device_id=device, device_id_type=MESH)
 
     @pl.when(z < 3)
@@ -61,7 +62,7 @@
         )
 
     above, below = jnp.where(z < 3, 1, 0), jnp.where(z > 0, 1, 0)
-    pl.semaphore_wait(barrier, 3 + above + below)
+    pl.semaphore_wait(barrier, len(near) + above + below)
 
 
 def halves(core):
@@ -719,20 +720,524 @@
     )(middle, cotangent, blended, output_full, vectors, full)
 
 
-def contract_rows(left_side, right_side):
-    return dot_tn(left_side, right_side)
-
-
-def norm_back(slope_rows, unit_rows, reciprocal, norm_gain):
-    tilted = slope_rows * norm_gain
-    centered_slope = tilted - jnp.mean(tilted, axis=-1, keepdims=True)
-    centered_slope = centered_slope - unit_rows * jnp.mean(
-        tilted * unit_rows, axis=-1, keepdims=True
-    )
-    return (
-        centered_slope * reciprocal,
-        jnp.sum(slope_rows * unit_rows, axis=0),
-        jnp.sum(slope_rows, axis=0),
+class Reduce:
+    def __init__(self, part, refs):
+        self.part = part
+        (
+            self.first_y, self.first_x, self.second_x, self.second_y, self.line_in,
+            self.first_sent, self.first_recv, self.second_sent, self.second_recv,
+            self.line_sent, self.line_recv,
+        ) = refs
+        core, x, y, z = place()
+        self.x, self.y, self.z = x, y, z
+        self.near_x, self.near_y = seat(core, 1 - x, y, z), seat(core, x, 1 - y, z)
+        self.above, self.below = seat(core, x, y, z + 1), seat(core, x, y, z - 1)
+
+    @staticmethod
+    def scratch(piece):
+        dma = pltpu.SemaphoreType.DMA
+        return [
+            pltpu.VMEM((4, 2) + piece, bf16), pltpu.VMEM((4, 2) + piece, bf16),
+            pltpu.VMEM((4,) + piece, bf16), pltpu.VMEM((4,) + piece, bf16),
+            pltpu.VMEM((2, 4, 2) + piece, bf16),
+            dma((4, 2)), dma((4, 2)), dma((4, 2)), dma((4, 2)), dma((2, 4, 2)), dma((2, 4, 2)),
+        ]
+
+    def first_copy(self, k, m):
+        sems = self.first_sent.at[k, m], self.first_recv.at[k, m]
+        if m == 0:
+            return remote(self.part.at[k, 0, 1 - self.y], self.first_y.at[k], *sems, self.near_y)
+        return remote(self.part.at[k, 1, :, 1 - self.x], self.first_x.at[k], *sems, self.near_x)
+
+    def second_copy(self, k, m):
+        x, y = self.x, self.y
+        sems = self.second_sent.at[k, m], self.second_recv.at[k, m]
+        if m == 0:
+            return remote(self.part.at[k, 0, y, 1 - x], self.second_x.at[k], *sems, self.near_x)
+        return remote(self.part.at[k, 1, 1 - y, x], self.second_y.at[k], *sems, self.near_y)
+
+    def line_copy(self, k, m, down):
+        return remote(
+            self.part.at[k, m, self.y, self.x], self.line_in.at[down, k, m],
+            self.line_sent.at[down, k, m], self.line_recv.at[down, k, m],
+            self.below if down else self.above,
+        )
+
+    def add_in(self, k, m, y_of, x_of, got):
+        old = self.part[k, m, y_of, x_of].astype(f32)
+        self.part[k, m, y_of, x_of] = (old + got.astype(f32)).astype(bf16)
+
+    def first(self, k):
+        for m in range(2):
+            self.first_copy(k, m).start()
+
+    def second(self, k):
+        x, y = self.x, self.y
+        self.first_copy(k, 0).wait_recv()
+        self.add_in(k, 0, y, 1 - x, self.first_y[k, 1 - x])
+        self.second_copy(k, 0).start()
+        self.first_copy(k, 1).wait_recv()
+        self.add_in(k, 1, 1 - y, x, self.first_x[k, 1 - y])
+        self.second_copy(k, 1).start()
+        self.add_in(k, 0, y, x, self.first_y[k, x])
+        self.add_in(k, 1, y, x, self.first_x[k, y])
+
+    def line(self, k):
+        for m, got in enumerate((self.second_x, self.second_y)):
+            self.second_copy(k, m).wait_recv()
+            self.add_in(k, m, self.y, self.x, got[k])
+        self.hop(k, 0)
+
+    def hop(self, k, hop):
+        x, y, z = self.x, self.y, self.z
+        for down, length, seat_z in ((0, k, hop), (1, 3 - k, 3 - hop)):
+            if hop < length:
+
+                @pl.when(z == seat_z)
+                def _():
+                    for m in range(2):
+                        if hop > 0:
+                            self.line_copy(k, m, down).wait_recv()
+                            self.add_in(k, m, y, x, self.line_in[down, k, m])
+                        self.line_copy(k, m, down).start()
+
+        if hop == max(k, 3 - k):
+
+            @pl.when(z == k)
+            def _():
+                for m in range(2):
+                    for down, length in ((0, k), (1, 3 - k)):
+                        if length > 0:
+                            self.line_copy(k, m, down).wait_recv()
+                            self.add_in(k, m, y, x, self.line_in[down, k, m])
+
+    def settle(self, k):
+        for m in range(2):
+            self.first_copy(k, m).wait_send()
+            self.second_copy(k, m).wait_send()
+            if k > 0:
+
+                @pl.when(self.z < k)
+                def _():
+                    self.line_copy(k, m, 0).wait_send()
+
+            if k < 3:
+
+                @pl.when(self.z > k)
+                def _():
+                    self.line_copy(k, m, 1).wait_send()
+
+
+class Gather:
+    def __init__(self, whole, refs):
+        self.whole = whole
+        self.recv, self.sent_x, self.sent_y, self.sent_z = refs
+        core, x, y, z = place()
+        self.x, self.y, self.z = x, y, z
+        self.near_x, self.near_y = seat(core, 1 - x, y, z), seat(core, x, 1 - y, z)
+        self.above, self.below = seat(core, x, y, z + 1), seat(core, x, y, z - 1)
+
+    @staticmethod
+    def scratch(piece):
+        dma = pltpu.SemaphoreType.DMA
+        return [
+            pltpu.VMEM((4, 2, 2, 2) + piece, bf16),
+            dma((4, 2, 2, 2)), dma((4, 2, 2)), dma((4, 2, 2)), dma((2, 4, 2)),
+        ]
+
+    def send(self, k, m, y_of, x_of, sem, device):
+        src = self.whole.at[k, m, y_of, x_of]
+        return remote(src, src, sem, self.recv.at[k, m, y_of, x_of], device)
+
+    def to_x(self, k, m, y_of):
+        return self.send(k, m, y_of, self.x, self.sent_x.at[k, m, y_of], self.near_x)
+
+    def to_y(self, k, m, x_of):
+        return self.send(k, m, self.y, x_of, self.sent_y.at[k, m, x_of], self.near_y)
+
+    def along(self, k, m, down):
+        device = self.below if down else self.above
+        return self.send(k, m, self.y, self.x, self.sent_z.at[down, k, m], device)
+
+    def arrived(self, k, m, y_of, x_of):
+        self.send(k, m, y_of, x_of, self.sent_x.at[k, m, 0], self.near_x).wait_recv()
+
+    def line(self, k, part):
+        x, y, z = self.x, self.y, self.z
+
+        @pl.when(z == k)
+        def _():
+            for m in range(2):
+                self.whole[k, m, y, x] = part[k, m, y, x]
+                if k < 3:
+                    self.along(k, m, 0).start()
+                if k > 0:
+                    self.along(k, m, 1).start()
+
+        @pl.when(z != k)
+        def _():
+            for m in range(2):
+                self.arrived(k, m, y, x)
+                if k < 2:
+
+                    @pl.when(jnp.logical_and(z > k, z < 3))
+                    def _():
+                        self.along(k, m, 0).start()
+
+                if k > 1:
+
+                    @pl.when(jnp.logical_and(z < k, z > 0))
+                    def _():
+                        self.along(k, m, 1).start()
+
+        self.to_x(k, 0, y).start()
+        self.to_y(k, 1, x).start()
+        self.to_x(k, 1, y).start()
+        self.to_y(k, 0, x).start()
+
+    def cross(self, k):
+        x, y = self.x, self.y
+        self.arrived(k, 0, y, 1 - x)
+        self.to_y(k, 0, 1 - x).start()
+        self.arrived(k, 1, 1 - y, x)
+        self.to_x(k, 1, 1 - y).start()
+
+    def rest(self, k):
+        x, y, z = self.x, self.y, self.z
+        self.arrived(k, 1, y, 1 - x)
+        self.arrived(k, 0, 1 - y, x)
+        for m in range(2):
+            self.arrived(k, m, 1 - y, 1 - x)
+            self.to_x(k, m, y).wait_send()
+            self.to_y(k, m, x).wait_send()
+            if k < 3:
+
+                @pl.when(jnp.logical_and(z >= k, z < 3))
+                def _():
+                    self.along(k, m, 0).wait_send()
+
+            if k > 0:
+
+                @pl.when(jnp.logical_and(z <= k, z > 0))
+                def _():
+                    self.along(k, m, 1).wait_send()
+
+        self.to_y(k, 0, 1 - x).wait_send()
+        self.to_x(k, 1, 1 - y).wait_send()
+
+
+BLOCKS = (
+    ((0, 0), (0, 1), (0, 2), (1, 0), (1, 1), (1, 2), (1, 3)),
+    ((0, 0), (0, 1), (0, 2), (0, 3), (1, 1), (1, 2), (1, 3)),
+)
+TRIPLE = HEADS // 4
+MIX_PIECE = (TRIPLE, 7, 16, 128)
+WEIGHT_PIECE = (48, HALF)
+
+
+def backward_kernel(
+    raised_ref, docs_ref, values_ref, blended_ref, share_ref, slope_ref, output_grad_ref, normed_ref,
+    value_ref, x_ref, middle_slope_ref, sums_ref, vector_ref,
+    inputs_out, mixing_out, weights_out, sums_out, *scratch,
+):
+    scratch = list(scratch)
+
+    def take(n):
+        got = scratch[:n]
+        del scratch[:n]
+        return got
+
+    mask, raised, chance, scaled, scaled_t, value_t, value_slope, grads = take(8)
+    half, mix_from, weights_to, weights_from, weights_part, small, small_in = take(7)
+    raised_sem, mix_sent, mix_recv, weights_sent, weights_recv, small_sent, small_recv = take(7)
+    mix_reduce_refs = take(11)
+    weights_reduce_refs = take(11)
+    mix_whole, *mix_gather_refs = take(5)
+    weights_whole, *weights_gather_refs = take(5)
+
+    core, x, y, z = place()
+    mine, other = halves(core)
+    twin = seat(1 - core, x, y, z)
+    tokens = x_ref.shape[0]
+    rows_count = tokens // SEQ
+    block = 256
+    order = (0, 3, 1, 2)
+    mix_part = half.at[core]
+    mix = Reduce(mix_part, mix_reduce_refs)
+    weights = Reduce(weights_part, weights_reduce_refs)
+    mix_all = Gather(mix_whole, mix_gather_refs)
+    weights_all = Gather(weights_whole, weights_gather_refs)
+
+    def load(h, buffer):
+        return pltpu.make_async_copy(raised_ref.at[h], raised.at[buffer], raised_sem.at[buffer])
+
+    load(order[0] * TRIPLE, 0).start()
+    pairs = (seat(core, x, y, z + 1 - 2 * lax.rem(z, 2)), seat(core, x, y, lax.rem(z + 2, 4)))
+    rounds = (twin, seat(core, 1 - x, y, z), seat(core, x, 1 - y, z)) + pairs
+    greet(core, x, y, z, (pairs[1],))
+    fill_mask(docs_ref, mask, rows_count)
+
+    def scale_pair(p, _):
+        lanes = pl.ds(pl.multiple_of(p * 128, 128), 128)
+        for r in range(rows_count):
+            rows = pl.ds(r * SEQ, SEQ)
+            low = (slope_ref[rows, lanes].astype(f32) * share_ref[rows, lanes]).astype(bf16)
+            scaled[rows, lanes] = low
+            scaled_t[lanes, rows] = low.T
+        return 0
+
+    lax.fori_loop(0, HEADS // 2, scale_pair, 0)
+
+    def head(k, first, last, n, _):
+        hh = n
+        h = k * TRIPLE + n
+        buffer = lax.rem(first + n, 2)
+        load(h, buffer).wait()
+
+        if last is None:
+
+            @pl.when(n < TRIPLE - 1)
+            def _():
+                load(h + 1, 1 - buffer).start()
+
+        else:
+            load(jnp.where(n < TRIPLE - 1, h + 1, last), 1 - buffer).start()
+
+        lanes = pl.ds(pl.multiple_of(lax.div(h, 2) * 128, 128), 128)
+        side = lax.rem(h, 2)
+        lane = lane_ids(SEQ)
+        inside = lax.div(lane, HEAD) == side
+        spot = lane - HEAD * (1 - side)
+        lefts, rights = [], []
+        for r in range(rows_count):
+            rows = pl.ds(r * SEQ, SEQ)
+            low = scaled[rows, lanes]
+            wide = low.astype(f32)
+            delta = jnp.sum(
+                jnp.where(inside, wide * blended_ref[rows, lanes].astype(f32), 0.0),
+                axis=-1, keepdims=True,
+            )
+            coarse = delta.astype(bf16).astype(f32)
+            fine = delta - coarse
+            extra = jnp.where(spot == 0, -coarse, jnp.where(spot == 1, -fine, 0.0))
+            lefts.append(jnp.where(inside, wide, extra).astype(bf16))
+            pair = values_ref[rows, lanes]
+            rights.append(jnp.where(inside, pair.astype(f32), 1.0).astype(bf16))
+        for i in range(0, SEQ, block):
+            total = None
+            for r in range(rows_count):
+                part = raised[buffer, i : i + block] * mask[r, i : i + block]
+                chance[r, i : i + block] = part
+                term = part.astype(f32) * dot_nt(lefts[r][i : i + block], rights[r])
+                total = term if total is None else total + term
+            total = total.astype(bf16)
+            for p, (row, column) in enumerate(BLOCKS[i // block]):
+                for q in range(8):
+                    start = row * 128 + q * 16
+                    half[i // block, k, q % 2, q // 4, (q // 2) % 2, hh, p] = total[
+                        start : start + 16, column * 128 : column * 128 + 128
+                    ]
+        for r in range(rows_count):
+            rows = pl.ds(pl.multiple_of(h * HEAD, HEAD), HEAD)
+            value_t[rows, r * SEQ : (r + 1) * SEQ] = dot_nn(
+                scaled_t[rows, r * SEQ : (r + 1) * SEQ], chance[r]
+            ).astype(bf16)
+        return 0
+
+    def mix_twin(k):
+        return remote(half.at[1 - core, k], mix_from.at[k], mix_sent.at[k], mix_recv.at[k], twin)
+
+    def mix_sum(k):
+        mix_twin(k).wait_recv()
+        for m in range(2):
+            for y_of in range(2):
+                for x_of in range(2):
+                    mix.add_in(k, m, y_of, x_of, mix_from[k, m, y_of, x_of])
+        mix.first(k)
+
+    for i in range(4):
+        k = order[i]
+        last = order[i + 1] * TRIPLE if i < 3 else None
+        lax.fori_loop(0, TRIPLE, functools.partial(head, k, TRIPLE * i, last), 0)
+        mix_twin(k).start()
+        if i >= 1:
+            mix_sum(order[i - 1])
+        if i >= 2:
+            (mix.second, mix.line)[i - 2](order[0])
+
+    def turn(p, _):
+        lanes = pl.ds(pl.multiple_of(p * 128, 128), 128)
+        value_slope[:, lanes] = value_t[lanes, :].T
+        return 0
+
+    lax.fori_loop(0, D // 128, turn, 0)
+    mix_sum(order[3])
+
+    def rows_of(b):
+        return pl.ds(pl.multiple_of(b * block, block), block)
+
+    def value_rows(b, _):
+        lanes = rows_of(b)
+        grads[lanes, :] = dot_tn(normed_ref[:, lanes], value_slope[...])
+        return 0
+
+    lax.fori_loop(0, D // block, value_rows, 0)
+    other_rows = pl.ds(pl.multiple_of((1 - core) * HALF, HALF), HALF)
+    my_rows = pl.ds(pl.multiple_of(core * HALF, HALF), HALF)
+    weights_to[0] = grads[:, other].astype(bf16)
+    for side in range(2):
+        weights_to[1, side * HALF : (side + 1) * HALF] = output_grad_ref[
+            other_rows, side * HALF : (side + 1) * HALF
+        ].astype(bf16)
+    weights_twin = remote(weights_to, weights_from, weights_sent, weights_recv, twin)
+    weights_twin.start()
+    small[0] = jnp.zeros_like(small[0])
+    small[0, 0:8] = sums_ref[...]
+    gain = vector_ref[0:1, :]
+
+    def finish(b, _):
+        rows = rows_of(b)
+        back = dot_nt(value_slope[rows, :], value_ref[...])
+        unit, reciprocal = unit_of(x_ref[rows, :].astype(f32))
+        small[0, 7:8, :] += jnp.sum(back * unit, axis=0, keepdims=True)
+        small[0, 8:9, :] += jnp.sum(back, axis=0, keepdims=True)
+        moved = middle_slope_ref[rows, :] + norm_slope(back, unit, reciprocal, gain)
+        inputs_out[rows, :] = moved.astype(bf16)
+        return 0
+
+    def small_copy(n):
+        return remote(small.at[n], small_in.at[n], small_sent.at[n], small_recv.at[n], rounds[n])
+
+    def small_sum(n):
+        small_copy(n).wait_recv()
+        small[n + 1] = small[n] + small_in[n]
+        if n + 1 < len(rounds):
+            small_copy(n + 1).start()
+
+    mix.second(order[1])
+    lax.fori_loop(0, 2, finish, 0)
+    mix.hop(order[0], 1)
+    lax.fori_loop(2, 4, finish, 0)
+    small_copy(0).start()
+    weights_twin.wait_recv()
+    share_rows = D // 4
+    for k in range(4):
+        rows = slice(k * share_rows, (k + 1) * share_rows)
+        own = pl.ds(pl.multiple_of(core * HALF + (k % 2) * share_rows, 64), share_rows)
+        side = slice((k // 2) * HALF, (k // 2 + 1) * HALF)
+        shape = (2, 2) + WEIGHT_PIECE
+        first = grads[rows, mine] + weights_from[0, rows].astype(f32)
+        weights_part[k, 0] = first.astype(bf16).reshape(shape)
+        second = output_grad_ref[own, side] + weights_from[1, rows].astype(f32)
+        weights_part[k, 1] = second.astype(bf16).reshape(shape)
+        weights.first(k)
+    mix.line(order[1])
+    small_sum(0)
+    mix.hop(order[0], 2)
+    mix.second(order[2])
+    mix.hop(order[1], 1)
+    small_sum(1)
+    mix.line(order[2])
+    mix.hop(order[0], 3)
+    mix_all.line(order[0], mix_part)
+    small_sum(2)
+    mix.hop(order[1], 2)
+    mix.second(order[3])
+    mix.hop(order[2], 1)
+    small_sum(3)
+    mix.line(order[3])
+    mix.hop(order[1], 3)
+    mix_all.line(order[1], mix_part)
+    small_sum(4)
+    mix.hop(order[2], 2)
+    mix_all.line(order[2], mix_part)
+    mix_all.cross(order[0])
+    mix.hop(order[3], 1)
+    for k in range(4):
+        weights.second(k)
+    mix.hop(order[3], 2)
+    mix_all.line(order[3], mix_part)
+    mix_all.cross(order[1])
+    for k in range(4):
+        weights.line(k)
+    mix_all.cross(order[2])
+    for k in range(4):
+        weights.hop(k, 1)
+    mix_all.cross(order[3])
+    for k in range(4):
+        weights.hop(k, 2)
+
+    def mixing_copy(k):
+        return pltpu.make_async_copy(mix_whole.at[k], mixing_out.at[k], raised_sem.at[2 + k])
+
+    mix_all.rest(order[0])
+    mixing_copy(order[0]).start()
+    for k in range(4):
+        weights.hop(k, 3)
+        weights_all.line(k, weights_part)
+    mix_all.rest(order[1])
+    mixing_copy(order[1]).start()
+    for k in range(4):
+        weights_all.cross(k)
+    for k in order[2:]:
+        mix_all.rest(k)
+        mixing_copy(k).start()
+    for k in range(4):
+        weights_all.rest(k)
+    weights_out[...] = weights_whole[...]
+    for n, row in enumerate((0, 1, 2, 7, 8)):
+        sums_out[n : n + 1, :] = small[5, row : row + 1, mine]
+    for n in range(4):
+        line = pl.ds(3 + 2 * core + n // 2, 1)
+        sums_out[5 + n : 6 + n, :] = small[5, line, (n % 2) * HALF : (n % 2 + 1) * HALF]
+    sums_out[9:16, :] = jnp.zeros((7, HALF), f32)
+    for n in range(5):
+        small_copy(n).wait_send()
+    weights_twin.wait_send()
+    for k in range(4):
+        mix_twin(k).wait_send()
+        mix.settle(k)
+        weights.settle(k)
+        mixing_copy(k).wait()
+
+
+def backward_call(
+    raised, documents, values, blended, share, slope, output_grad, normed, value_full, x,
+    middle_slope, sums, vectors,
+):
+    tokens = x.shape[0]
+    rows = tokens // SEQ
+    any_spec = pl.BlockSpec(memory_space=pl.ANY)
+    vmem = pl.BlockSpec(memory_space=pltpu.VMEM)
+    shape = jax.ShapeDtypeStruct
+    dma = pltpu.SemaphoreType.DMA
+    return pl.pallas_call(
+        backward_kernel,
+        out_shape=(
+            shape((tokens, D), bf16), shape((4, 2, 2, 2) + MIX_PIECE, bf16),
+            shape((4, 2, 2, 2) + WEIGHT_PIECE, bf16), shape((16, HALF), f32),
+        ),
+        in_specs=[any_spec] + [vmem] * 12,
+        out_specs=[vmem, any_spec, vmem, vmem],
+        scratch_shapes=[
+            pltpu.VMEM((rows, SEQ, SEQ), bf16), pltpu.VMEM((2, SEQ, SEQ), bf16),
+            pltpu.VMEM((rows, SEQ, SEQ), bf16), pltpu.VMEM((tokens, D), bf16),
+            pltpu.VMEM((D, tokens), bf16), pltpu.VMEM((D, tokens), bf16),
+            pltpu.VMEM((tokens, D), bf16), pltpu.VMEM((D, D), f32),
+            pltpu.VMEM((2, 4, 2, 2, 2) + MIX_PIECE, bf16), pltpu.VMEM((4, 2, 2, 2) + MIX_PIECE, bf16),
+            pltpu.VMEM((2, D, HALF), bf16), pltpu.VMEM((2, D, HALF), bf16),
+            pltpu.VMEM((4, 2, 2, 2) + WEIGHT_PIECE, bf16),
+            pltpu.VMEM((6, 16, D), f32), pltpu.VMEM((5, 16, D), f32),
+            dma((6,)), dma((4,)), dma((4,)), dma, dma, dma((5,)), dma((5,)),
+            *Reduce.scratch(MIX_PIECE), *Reduce.scratch(WEIGHT_PIECE),
+            *Gather.scratch(MIX_PIECE), *Gather.scratch(WEIGHT_PIECE),
+        ],
+        compiler_params=pltpu.CompilerParams(
+            collective_id=2, has_side_effects=True, vmem_limit_bytes=62 << 20
+        ),
+    )(
+        raised, documents, values, blended, share, slope, output_grad, normed, value_full, x,
+        middle_slope, sums, vectors,
     )
 
 
@@ -752,68 +1257,34 @@
     ) = forward_call(
         inputs.reshape(tokens, D), documents, mixing, value_weight, output_weight, shard, vectors
     )
-    gain_first = vector_full[0]
-    stream = inputs.reshape(tokens, D).astype(f32)
-    unit_first, recip_first = unit_of(stream)
     (
         result, middle_slope, blended_slope, output_grad, sums_two, hidden_share, down_share,
     ) = dense_call(middle, cotangent.reshape(tokens, D), blended, output_full, vector_full, full)
     hidden_share = hidden_share.T
-    down_bias_sum, gain_second_sum, shift_second_sum = (sums_two[n] for n in range(3))
-    hidden_bias_sum = sums_two[3:7].reshape(FF)
-    value_rows = values.reshape(row_count, SEQ, D)
-
-    def mix_back(running, bundle):
-        row_values, row_docs, row_slope = bundle
-        same = row_docs[:, None] == row_docs[None, :]
-        chances = jnp.where(same[None], raised.astype(f32), 0.0)
-        chances = chances / jnp.sum(chances, axis=-1, keepdims=True)
-        per_head = row_values.reshape(SEQ, HEADS, HEAD)
-        head_slope = row_slope.reshape(SEQ, HEADS, HEAD)
-        chance_slope = jnp.einsum(
-            "ihd,jhd->hij", head_slope, per_head, preferred_element_type=jnp.float32
-        )
-        score_slope = chances * (
-            chance_slope - jnp.sum(chances * chance_slope, axis=-1, keepdims=True)
-        )
-        value_part = jnp.einsum(
-            "hij,ihd->jhd",
-            chances.astype(jnp.bfloat16),
-            head_slope,
-            preferred_element_type=jnp.float32,
-        )
-        return (running + score_slope, value_part.reshape(SEQ, D).astype(jnp.bfloat16))
-
-    mixing_start = jnp.zeros((HEADS, SEQ, SEQ), jnp.float32)
-    mixing_grad, value_slopes = lax.scan(
-        mix_back, mixing_start, (value_rows, documents, blended_slope.reshape(row_count, SEQ, D))
-    )
-    value_slope = value_slopes.reshape(tokens, D)
-    value_grad = contract_rows(normed_low, value_slope)
-    normed_slope = dot_nt(value_slope, value_full)
-    back_first, gain_first_sum, shift_first_sum = norm_back(
-        normed_slope, unit_first, recip_first, gain_first
-    )
-    inputs_slope = (middle_slope + back_first).astype(jnp.bfloat16)
-
-    def scatter(array, axis_name, axis):
-        return lax.psum_scatter(
-            array.astype(bf16), axis_name, scatter_dimension=axis, tiled=True
-        ).astype(f32)
-
-    sums = (
-        (mixing_grad, 1), (value_grad, 1), (output_grad, 0), (gain_first_sum, 0),
-        (shift_first_sum, 0), (gain_second_sum, 0), (shift_second_sum, 0), (hidden_bias_sum, 0),
-        (down_bias_sum, 0),
-    )
-    totals = [
-        lax.psum(scatter(one, "narrow", axis).astype(bf16), "wide").astype(f32)
-        for one, axis in sums
-    ]
+    inputs_slope, mixing_packed, weights_packed, sums = backward_call(
+        raised, documents, values, blended, share, blended_slope, output_grad, normed_low,
+        value_full, inputs.reshape(tokens, D), middle_slope, sums_two, vector_full,
+    )
+    blocks = mixing_packed.transpose(0, 4, 5, 2, 3, 1, 6, 7).reshape(HEADS, 7, 128, 128)
+    blocks = blocks.astype(f32)
+    nothing = jnp.zeros((HEADS, 128, 128), f32)
+
+    def lay(half):
+        found = {spot: blocks[:, n] for n, spot in enumerate(BLOCKS[half])}
+        rows = [
+            jnp.concatenate([found.get((row, column), nothing) for column in range(4)], axis=2)
+            for row in range(2)
+        ]
+        return jnp.concatenate(rows, axis=1)
+
+    mixing_grad = jnp.where(lax.axis_index("narrow") == 0, lay(0), lay(1))
+    value_grad = weights_packed[:, 0].reshape(D, HALF).astype(f32)
+    output_grad = weights_packed[:, 1].reshape(2, HALF, HALF).swapaxes(0, 1).reshape(HALF, D)
+    shape = inputs.shape
     return (
-        result.reshape(row_count, SEQ, D),
-        inputs_slope.reshape(row_count, SEQ, D),
-        *totals[:7], hidden_share, totals[7], down_share, totals[8],
+        result.reshape(shape), inputs_slope.reshape(shape), mixing_grad, value_grad,
+        output_grad.astype(f32), sums[3], sums[4], sums[1], sums[2], hidden_share,
+        sums[5:9].reshape(4 * HALF), down_share, sums[0],
     )
 
 

time: 473 us -> 302 us (0.64)
  waiting for transfers between devices: 148 us -> 0 us
  Pallas kernels: 132 us -> 272 us
  matrix products: 52.4 us -> 0 us
  blocking collectives: 49.6 us -> 0 us
  local copies, waits for them, and re-layouts: 39.8 us -> 13 us
  other arithmetic: 28.6 us -> 10.6 us
  between operations: 15.5 us -> 1.19 us
    pallas_call x0 -> x1, Pallas kernels: none -> 140 us  [backward_call(): pl.pallas_call(backward_kernel, out_shape=(shape((tokens, D), bf16), shap...]
    psum x1 -> x0, waiting for transfers between devices: 117 us -> none  [local(): lax.psum(scatter(one, 'narrow', axis).astype(bf16), 'wide').astype(f32)]
    psum x1 -> x0, blocking collectives: 46.2 us -> none  [local(): lax.psum(scatter(one, 'narrow', axis).astype(bf16), 'wide').astype(f32)]
    sub x2 -> x0, matrix products: 34.1 us -> none  [mix_back(): chance_slope - jnp.sum(chances * chance_slope, axis=-1, keepdims=True)]
    reduce_scatter x2 -> x0, waiting for transfers between devices: 29.3 us -> none  [scatter(): lax.psum_scatter(array.astype(bf16), axis_name, scatter_dimension=axis, t...]
    dot_general x4 -> x0, matrix products: 18.3 us -> none  [the longest x2 10.2 us: mix_back(): jnp.einsum('hij,ihd->jhd', chances.astype(jnp.bfloat16), head_slope, pref...]
    convert_element_type x11 -> x2, other arithmetic: 16.7 us -> 3.59 us  [the longest x1 2.44 us: local(): blocks = blocks.astype(f32)]
    unnamed x37 -> x16, local copies, waits for them, and re-layouts: 16.4 us -> 3.74 us
  transfers between devices with their start and end apart: 4 -> 0, of which waited for: 4 -> 0; matrix products, arithmetic and copies ran while one was open for 6% -> 0% of each run, Pallas kernels for 0% -> 0%
where the time goes in v3:
time: 302 us; the launch traced here: 297 us
  Pallas kernels  272 us (90%)
  local copies, waits for them, and re-layouts  13 us (4%)
  other arithmetic  10.6 us (4%)
    pallas_call x1, Pallas kernels, backward_call(): pl.pallas_call(backward_kernel, out_shape=(shape((tokens, D), bf16), shap...  140 us
    pallas_call x1, Pallas kernels, dense_call(): pl.pallas_call(dense_kernel, out_shape=(shape((tokens, D), bf16), shape((...  73.5 us
    pallas_call x1, Pallas kernels, forward_call(): pl.pallas_call(forward_kernel, out_shape=(shape((2, FF, D), bf16), shape(...  58.9 us

profile of v3, /device:TPU:0, one launch (start us, length us, event | category | flops | bytes accessed | tf_op | source)
XLA Modules:
  0.0 296.9 jit_solution(13838124625355253791)
XLA Ops:
  0.6 1.7 pad_maximum_fusion.7.shard_ref
  2.4 0.7 reshape.56
  3.1 0.7 stack.27
  3.8 0.7 stack.28
  4.4 0.7 stack.29
  5.1 0.7 stack.30
  5.8 0.7 stack.31
  6.5 0.1 concatenate.21
  6.6 0.6 convert_element_type.30.vector_ref
  7.3 58.9 %shard_map.237 = (bf16[2,3072,768]{2,1,0:T(8,128)(2,1)}, bf16[12,512,512]{2,1,0:T(8,128)(2,1)}, bf16[768,768]{1,0:T(8,128)(2,1)}, bf16[768,768]{1,0:T(8,128)(2,1...) custom-call(bf16[1024,768]{1,0:T(8,128)(2,1)} %bitcast.48, ...), custom_call_target="tpu_custom_call" | custom-call | tf_op jit(solution)/shard_map/pallas_call | solution.py:386
  66.1 73.5 %shard_map.238 = (bf16[1024,768]{1,0:T(8,128)(2,1)}, f32[1024,768]{1,0:T(8,128)}, bf16[1024,768]{1,0:T(8,128)(2,1)}, f32[768,768]{1,0:T(8,128)}, f32[8,768]{1,0:...) custom-call(f32[1024,768]{1,0:T(8,128)} %get-tuple-element.34.middle_ref, bf16[1024,768]{1,0:T(8,128)(2,1)} %bitcast.51, ...), custom_call_target="tpu_custom_call" | custom-call | tf_op jit(solution)/shard_map/pallas_call | solution.py:696
  139.7 139.8 %shard_map.239 = (bf16[1024,768]{1,0:T(8,128)(2,1)}, bf16[4,2,2,2,3,7,16,128]{7,6,5,4,3,2,1,0:T(8,128)(2,1)}, bf16[4,2,2,2,48,384]{5,4,3,2,1,0:T(8,128)(2,1)}, f32[16,384]{1,0:T(8,128)}) custom-call(bf16[12,512,512]{2,1,0:T(8,128)(2,1)} %get-tuple-element.40.raised_ref, s32[2,512]{1,0:T(2,128)} %docs_ref.3, bf16[1024,768]{1,0:T(8,128)(2,1)} %get-tuple-element.41.values_ref, ...), custom_call_target="tpu_custom_call" | custom-call | tf_op jit(solution)/shard_map/pallas_call | solution.py:1214
  279.4 2.4 convert_bitcast_fusion
  281.9 0.9 copy.28
  282.7 1.6 slice_bitcast_fusion.6
  284.3 0.1 broadcast_in_dim.7
  284.4 0.0 copy-start.2
  284.4 4.6 %fusion.1 = f32[12,256,512]{2,1,0:T(8,128)} fusion(f32[12,128,128]{2,1,0:T(8,128)} %get-tuple-element.65, f32[12,128,128]{2,1,0:T(8,128)} %get-tuple-element.66, f32[12,128,128]{2,1,0:T(8,128)S(1)} %get-tuple-element.61, f32[12,128,128]{2,1,0:T(8,128)S(1)} %get-tuple-element.62, f32[12,128,128]{2,1,0:T(8,128)S(1)} %broadcast_in_dim.7, ...), kind=kLoop, calls=%fused_computation.7 | loop fusion | flops 20447232 | bytes 12582913 | tf_op jit(solution)/shard_map/jit(_where)/select_n | solution.py:1280
  289.0 0.0 copy-done.2
  289.0 0.0 copy-start.1
  289.0 0.1 fusion.4
  289.2 0.1 convert_bitcast_fusion.1
  289.3 1.1 copy.42
  290.4 1.1 bitcast_convert_fusion
  291.5 0.0 copy-done.5
  291.5 0.6 reshape.60
  292.1 0.6 slice_reduce_fusion
  292.7 1.1 copy.47
  293.9 0.0 copy-done.1
  293.9 1.1 copy.48
  295.0 0.7 copy.49
  295.8 0.7 copy.50
  (9 shorter events, 0.0 us)
Async XLA Ops:
  284.4 4.6 %copy-start.2 = (bf16[4,2,2,2,48,384]{5,4,3,2,1,0:T(8,128)(2,1)S(1)}, bf16[4,2,2,2,48,384]{5,4,3,2,1,0:T(8,128)(2,1)}, u32[]{:S(2)}) copy-start(bf16[4,2,2,2,48,384]{5,4,3,2,1,0:T(8,128)(2,1)} %get-tuple-element.51) | copy-start | bytes 3538948
  289.0 2.5 copy-start.5
  289.0 3.7 %copy-start = (bf16[1024,768]{1,0:T(8,128)(2,1)S(1)}, bf16[1024,768]{1,0:T(8,128)(2,1)}, u32[]{:S(2)}) copy-start(bf16[1024,768]{1,0:T(8,128)(2,1)} %get-tuple-element.39) | copy-start | bytes 4718596
  289.0 4.9 %copy-start.1 = (bf16[1024,768]{1,0:T(8,128)(2,1)S(1)}, bf16[1024,768]{1,0:T(8,128)(2,1)}, u32[]{:S(2)}) copy-start(bf16[1024,768]{1,0:T(8,128)(2,1)} %get-tuple-element.49) | copy-start | bytes 4718596
  289.3 6.5 %copy-start.3 = (f32[192,384]{1,0:T(8,128)S(1)}, f32[192,384]{1,0:T(8,128)}, u32[]{:S(2)}) copy-start(f32[192,384]{1,0:T(8,128)} %get-tuple-element.93) | copy-start | bytes 884740
  292.1 2.9 copy-start.4
